TPU v7x, 128 devices: a whole 4x4x4 slice. The times are simulated.
128 devices in a mesh: dp: 8 (over y, core), fsdp: 16 (over z, x).
Axes of the slice: x: 4, y: 4, z: 4, core: 2. Of those that a mesh axis runs over, the one named last changes fastest.
Arguments:
- waveforms: bfloat16 [8, 2048, 320], P('dp', 'fsdp'), may hold values from -6 to 6
- packing_list: int32 [4, 2048], P(None, 'fsdp'), may hold values from 0 to 128, as said below
- segment_ids: int32 [8, 2048], P('dp', 'fsdp'), may hold values from -1 to 127, as said below
- first_weight: bfloat16 [512, 10], P('fsdp'), may hold values from -2 to 2
- first_bias: bfloat16 [512], P('fsdp'), may hold values from -3 to 3
- first_gain: bfloat16 [512], P('fsdp'), may hold values from 0.5 to 1.5
- first_shift: bfloat16 [512], P('fsdp'), may hold values from -3 to 3
- second_weight: bfloat16 [512, 1536], P('fsdp'), may hold values from -0.15625 to 0.15625
- second_bias: bfloat16 [512], P('fsdp'), may hold values from -3 to 3
- second_gain: bfloat16 [512], P('fsdp'), may hold values from 0.5 to 1.5
- second_shift: bfloat16 [512], P('fsdp'), may hold values from -3 to 3
- cotangent: bfloat16 [8, 65536, 512], P('dp', 'fsdp'), may hold values from -0.01171875 to 0.01171875
Outputs:
- features: bfloat16 [8, 65536, 512], P('dp', 'fsdp')
- first_weight_grad: float32 [512, 10], P('fsdp')
- first_bias_grad: float32 [512], P('fsdp')
- first_gain_grad: float32 [512], P('fsdp')
- first_shift_grad: float32 [512], P('fsdp')
- second_weight_grad: float32 [512, 1536], P('fsdp')
- second_bias_grad: float32 [512], P('fsdp')
- second_gain_grad: float32 [512], P('fsdp')
- second_shift_grad: float32 [512], P('fsdp')
Inputs may be any that keep to these rules, and one draw needn't show every extreme that they name: `packing_list`: columns j * 128 to (j + 1) * 128 - 1 are the list of fsdp index j, the same for every dp index. Rows: source reader (a dp index), owner (a dp index), frame offset in the owner's packed sequence, length in frames (0 for an empty entry, whose offset is 128). Entries come two for each (reader, owner) pair, in shuffled order. A reader sends at most 16 frames to one owner; in every column one reader sends exactly 16 frames to every owner and one owner receives exactly 16 frames from every reader. An owner's utterances do not intersect and end within its 128 frames. `segment_ids`: the list index of the utterance covering each frame of an owner's packed sequence, -1 where none does.
All inputs are finite; a program needn't handle non-finite values.
Results may differ from a plain program's by a relative error of at most 0.0055.
Values may be sent and summed in bfloat16 or wider, within the bound.
A program may use at most 256 MiB of HBM per device.

v0:
```python
from functools import partial

import jax
import jax.numpy as jnp
from jax import lax
from jax.sharding import PartitionSpec as P

epsilon = 1e-05


def norm_act(pre_act, scale_by, shift_by, keep_rows):
    average = jnp.mean(pre_act, axis=-1, keepdims=True)
    centred = pre_act - average
    spread = jnp.mean(centred * centred, axis=-1, keepdims=True)
    scaled = centred * lax.rsqrt(spread + epsilon) * scale_by + shift_by
    return jax.nn.gelu(scaled, approximate=False) * keep_rows[:, None]


def frame_masks(segment, per_frame):
    following = jnp.concatenate([segment[1:], jnp.full((1,), -1, jnp.int32)])
    ending = following != segment
    places = jnp.arange(per_frame, dtype=jnp.int32)
    keeping = (segment >= 0)[:, None] & jnp.logical_not(
        ending[:, None] & (places == per_frame - 1)[None, :]
    )
    return keeping.reshape(-1).astype(jnp.float32)


def list_offsets(source, owner_of, length):
    ordinal = jnp.arange(source.shape[0], dtype=jnp.int32)
    earlier = ordinal[None, :] < ordinal[:, None]
    same_source = source[None, :] == source[:, None]
    same_pair = same_source & (owner_of[None, :] == owner_of[:, None])
    read_at = jnp.sum(jnp.where(earlier & same_source, length[None, :], 0), axis=1)
    slot_at = jnp.sum(jnp.where(earlier & same_pair, length[None, :], 0), axis=1)
    return (read_at, slot_at)


def local_pass(packed, segment, params, cotangent_block):
    kernel_one, bias_one, gain_one, shift_one, kernel_two, bias_two, gain_two, shift_two = params
    channels = kernel_two.shape[0]
    keep_first = frame_masks(segment, 64)
    keep_second = frame_masks(segment, 32)
    blocks = packed.reshape(-1, 5)
    following = jnp.concatenate([blocks[1:], jnp.zeros((1, 5), blocks.dtype)])
    patches = jnp.concatenate([blocks, following], axis=1)
    pre_first = lax.dot_general(
        patches, kernel_one, (((1,), (1,)), ((), ())), preferred_element_type=jnp.float32
    )
    pre_first = pre_first + bias_one.astype(jnp.float32)
    post_first, back_first = jax.vjp(
        partial(norm_act, keep_rows=keep_first),
        pre_first,
        gain_one.astype(jnp.float32),
        shift_one.astype(jnp.float32),
    )
    hidden = post_first.astype(jnp.bfloat16)
    paired = hidden.reshape(-1, 2 * channels)
    next_row = jnp.concatenate([paired[1:, :channels], jnp.zeros((1, channels), jnp.bfloat16)])
    columns = jnp.concatenate([paired, next_row], axis=1)
    pre_second = lax.dot_general(
        columns, kernel_two, (((1,), (1,)), ((), ())), preferred_element_type=jnp.float32
    )
    pre_second = pre_second + bias_two.astype(jnp.float32)
    post_second, back_second = jax.vjp(
        partial(norm_act, keep_rows=keep_second),
        pre_second,
        gain_two.astype(jnp.float32),
        shift_two.astype(jnp.float32),
    )
    features = post_second.astype(jnp.bfloat16)
    grad_pre_two, grad_gain_two, grad_shift_two = back_second(cotangent_block.astype(jnp.float32))
    grad_bias_two = jnp.sum(grad_pre_two, axis=0)
    grad_second = grad_pre_two.astype(jnp.bfloat16)
    grad_columns = jnp.dot(grad_second, kernel_two, preferred_element_type=jnp.float32)
    shifted = jnp.concatenate(
        [jnp.zeros((1, channels), jnp.float32), grad_columns[:-1, 2 * channels :]]
    )
    grad_hidden = (
        grad_columns[:, : 2 * channels]
        + jnp.concatenate([shifted, jnp.zeros_like(shifted)], axis=1)
    ).reshape(-1, channels)
    grad_pre_one, grad_gain_one, grad_shift_one = back_first(grad_hidden)
    grad_bias_one = jnp.sum(grad_pre_one, axis=0)
    grad_first = grad_pre_one.astype(jnp.bfloat16)
    grad_kernel_one = lax.dot_general(
        grad_first, patches, (((0,), (0,)), ((), ())), preferred_element_type=jnp.float32
    )
    smalls = (
        grad_kernel_one,
        grad_bias_one,
        grad_gain_one,
        grad_shift_one,
        grad_bias_two,
        grad_gain_two,
        grad_shift_two,
    )
    return (features, grad_second, columns, smalls)


def local(
    waveforms,
    packing_list,
    segment_ids,
    first_weight,
    first_bias,
    first_gain,
    first_shift,
    second_weight,
    second_bias,
    second_gain,
    second_shift,
    cotangent,
):
    group_count = lax.axis_size("dp")
    own_index = lax.axis_index("dp")
    frames = waveforms.shape[1]
    source = packing_list[0]
    owner_of = packing_list[1]
    place_at = packing_list[2]
    length = packing_list[3]
    read_at, slot_at = list_offsets(source, owner_of, length)
    position = jnp.arange(frames, dtype=jnp.int32)[:, None]
    covered = (
        (owner_of[None, :] == own_index)
        & (position >= place_at[None, :])
        & (position < (place_at + length)[None, :])
    )
    filled = jnp.any(covered, axis=1)
    readers = lax.all_gather(waveforms, "dp", axis=0, tiled=True).reshape(group_count * frames, 320)
    base_row = source * frames + read_at
    pick_rows = jnp.sum(
        jnp.where(covered, base_row[None, :] + position - place_at[None, :], 0), axis=1
    )
    packed = jnp.where(filled[:, None], readers[pick_rows], 0)
    params = (
        lax.all_gather(first_weight, "fsdp", axis=0, tiled=True),
        lax.all_gather(first_bias, "fsdp", axis=0, tiled=True),
        lax.all_gather(first_gain, "fsdp", axis=0, tiled=True),
        lax.all_gather(first_shift, "fsdp", axis=0, tiled=True),
        lax.all_gather(second_weight, "fsdp", axis=0, tiled=True),
        lax.all_gather(second_bias, "fsdp", axis=0, tiled=True),
        lax.all_gather(second_gain, "fsdp", axis=0, tiled=True),
        lax.all_gather(second_shift, "fsdp", axis=0, tiled=True),
    )
    features, grad_second, columns, smalls = local_pass(
        packed, segment_ids[0], params, cotangent[0]
    )
    second_part = lax.psum_scatter(
        lax.dot_general(
            grad_second, columns, (((0,), (0,)), ((), ())), preferred_element_type=jnp.float32
        ),
        "fsdp",
        scatter_dimension=0,
        tiled=True,
    )
    summed = (
        lax.psum_scatter(smalls[0], "fsdp", scatter_dimension=0, tiled=True),
        lax.psum_scatter(smalls[1], "fsdp", scatter_dimension=0, tiled=True),
        lax.psum_scatter(smalls[2], "fsdp", scatter_dimension=0, tiled=True),
        lax.psum_scatter(smalls[3], "fsdp", scatter_dimension=0, tiled=True),
        lax.psum_scatter(smalls[4], "fsdp", scatter_dimension=0, tiled=True),
        lax.psum_scatter(smalls[5], "fsdp", scatter_dimension=0, tiled=True),
        lax.psum_scatter(smalls[6], "fsdp", scatter_dimension=0, tiled=True),
    )
    results = lax.psum(
        (second_part, summed[0], summed[1], summed[2], summed[3], summed[4], summed[5], summed[6]),
        "dp",
    )
    return (
        features[None],
        results[1],
        results[2],
        results[3],
        results[4],
        results[0],
        results[5],
        results[6],
        results[7],
    )


def solution(mesh):
    placed = (
        P("dp", "fsdp", None),
        P(None, "fsdp"),
        P("dp", "fsdp"),
        P("fsdp", None),
        P("fsdp"),
        P("fsdp"),
        P("fsdp"),
        P("fsdp", None),
        P("fsdp"),
        P("fsdp"),
        P("fsdp"),
        P("dp", "fsdp", None),
    )
    return jax.shard_map(
        local,
        mesh=mesh,
        in_specs=placed,
        out_specs=(
            P("dp", "fsdp", None),
            P("fsdp", None),
            P("fsdp"),
            P("fsdp"),
            P("fsdp"),
            P("fsdp", None),
            P("fsdp"),
            P("fsdp"),
            P("fsdp"),
        ),
        check_vma=False,
    )
```

profile of v0, /device:TPU:1, one launch (start us, length us, event | category | flops | bytes accessed | tf_op | source)
XLA Modules:
  0.0 529.7 jit_solution(12288807466900540374)
XLA Ops:
  10.9 15.3 %all_gather.27 = bf16[8,128,320]{1,2,0:T(8,128)(2,1)S(1)} all-gather(bf16[1,128,320]{1,2,0:T(8,128)(2,1)} %param.12), channel_id=1, replica_groups=mesh['dp'=8,'fsdp'=16] {'dp'}, dimensions={0}, use_global_device_ids=true | all-gather | bytes 737280 | tf_op jit(solution)/shard_map/all_gather | solution.py:130
  27.4 5.6 %gather.6 = bf16[8192,5]{1,0:T(8,128)(2,1)} reshape(bf16[128,320]{1,0:T(8,128)(2,1)S(1)} %gather_fusion) | data formatting | bytes 163840 | tf_op jit(solution)/shard_map/gather | solution.py:135
  33.0 5.8 %broadcast_select_fusion = bf16[8192,5]{1,0:T(8,128)(2,1)S(1)} fusion(bf16[8192,5]{1,0:T(8,128)(2,1)} %gather.6, pred[8192]{0:T(1024)(128)(4,1)S(1)} %broadcast_in_dim.43), kind=kLoop, calls=%fused_computation.70 | loop fusion | flops 40960 | bytes 172032 | tf_op jit(solution)/shard_map/jit(_where)/select_n | solution.py:135
  44.5 35.0 %all-reduce.18 = (bf16[512]{0:T(512)(128)(2,1)S(1)}, bf16[512]{0:T(512)(128)(2,1)S(1)}, bf16[512]{0:T(512)(128)(2,1)S(1)}, bf16[512]{0:T(512)(128)(2,1)S(1)}, bf...) all-reduce(bf16[512]{0:T(512)(128)(2,1)S(1)} %dynamic-update-slice.5,, ...), channel_id=1, replica_groups=mesh['dp'=8,'fsdp'=16] {'fsdp'}, use_global_device_ids=true, to_apply=%add.9 | all-reduce | flops 3072 | bytes 12288
  79.8 15.4 %all-gather = bf16[16,32,10]{1,2,0:T(8,128)(2,1)S(1)} all-gather(bf16[1,32,10]{1,2,0:T(8,128)(2,1)S(1)} %bitcast.44), channel_id=1, replica_groups=mesh['dp'=8,'fsdp'=16] {'fsdp'}, dimensions={0}, use_global_device_ids=true | all-gather | bytes 10880 | tf_op jit(solution)/shard_map/all_gather | solution.py:137
  97.5 8.1 %add_reduce_fusion.1 = (f32[8192]{0:T(1024)S(1)}, f32[8192,512]{0,1:T(8,128)}) fusion(f32[512]{0:T(512)S(1)} %convert_element_type.58, bf16[512,10]{0,1:T(8,128)(2,1)S(1)} %reshape.230, bf16[8191,5]{0,1:T(8,128)(2,1)S(1)} %copy.57, bf16[8192,5]{0,1:T(8,128)(2,1)S(1)} %copy.47), kind=kOutput, calls=%fused_computation.29 | convolution fusion | flops 92758016 | bytes 16986102 | tf_op jit(solution)/shard_map/dot_general | solution.py:47
  105.6 8.6 %multiply_reduce_fusion.2 = f32[8192]{0:T(1024)S(1)} fusion(f32[8192]{0:T(1024)S(1)} %broadcast_multiply_fusion, f32[8192,512]{0,1:T(8,128)} %get-tuple-element.98, f32[512]{0:T(512)S(1)} %convert_element_type.58), kind=kLoop, calls=%fused_computation.24 | loop fusion | flops 16769024 | bytes 16844800 | tf_op jit(solution)/shard_map/jvp()/reduce_sum | solution.py:14
  114.2 43.1 %multiply_convert_fusion = (bf16[8192,512]{0,1:T(8,128)(2,1)}, f32[8192,512]{0,1:T(8,128)}) fusion(f32[8192]{0:T(1024)S(1)} %reshape.200, f32[512]{0:T(512)S(1)} %convert_element_type.60, f32[512]{0:T(512)S(1)} %convert_element_type.59, f32[8192]{0:T(1024)S(1)} %fusion.39, f32[8192]{0:T(1024)S(1)} %broadcast_multiply_fusion, ...), kind=kLoop, calls=%fused_computation.10 | loop fusion | flops 297795584 | bytes 42047488 | tf_op jit(solution)/shard_map/convert_element_type | solution.py:57
  157.7 6.4 %copy.52 = bf16[1,4096,512]{1,2,0:T(8,128)(2,1)} copy(bf16[1,4096,512]{2,1,0:T(8,128)(2,1)} %param.23) | data formatting | bytes 8388608 | tf_op args[11]
  164.1 11.9 %copy.50 = bf16[8192,512]{1,0:T(8,128)(2,1)} copy(bf16[8192,512]{0,1:T(8,128)(2,1)} %get-tuple-element.86) | data formatting | bytes 16777216 | tf_op jit(solution)/shard_map/convert_element_type | solution.py:57
  176.0 13.3 %reshape.198 = bf16[4096,1024]{1,0:T(8,128)(2,1)} reshape(bf16[8192,512]{1,0:T(8,128)(2,1)} %copy.50) | data formatting | bytes 16777216 | tf_op jit(solution)/shard_map/reshape | solution.py:58
  189.3 5.3 slice.41
  195.3 9.9 %add_reduce_fusion.3 = (f32[4096]{0:T(1024)S(1)}, f32[4096,512]{0,1:T(8,128)S(1)}) fusion(f32[512]{0:T(512)S(1)} %convert_element_type.64, bf16[512,1536]{1,0:T(8,128)(2,1)} %all-gather.3.cloned.1.call-done, bf16[4095,512]{1,0:T(8,128)(2,1)} %slice.41, bf16[4096,1024]{1,0:T(8,128)(2,1)} %reshape.198), kind=kOutput, calls=%fused_computation.66 | convolution fusion | flops 6484389888 | bytes 22561792 | tf_op jit(solution)/shard_map/dot_general | solution.py:61
  207.4 27.5 %multiply_reduce_fusion.3 = (f32[512]{0:T(512)S(1)}, f32[4096]{0:T(1024)S(1)}, f32[512]{0:T(512)S(1)}, f32[4096,512]{0,1:T(8,128)}, f32[4096,512]{0,1:T(8,128)}) fusion(f32[4096]{0:T(1024)S(1)} %fusion.40, f32[4096]{0:T(1024)S(1)} %broadcast_multiply_fusion.1, f32[4096,512]{0,1:T(8,128)S(1)} %get-tuple-element.100, f32[512]{0:T(512)S(1)} %convert_element_type.64, ...), kind=kLoop, calls=%fused_computation.44 | loop fusion | flops 176155648 | bytes 29435904 | tf_op jit(solution)/shard_map/transpose(jvp())/reduce_sum | solution.py:15
  234.8 10.0 %fusion.56 = (f32[4096]{0:T(1024)S(1)}, f32[4096,512]{0,1:T(8,128)S(1)}, bf16[1,4096,512]{1,2,0:T(8,128)(2,1)}) fusion(f32[4096]{0:T(1024)S(1)} %multiply_multiply_fusion.11, f32[4096]{0:T(1024)S(1)} %broadcast_multiply_fusion.1, f32[4096,512]{0,1:T(8,128)S(1)} %get-tuple-element.100, f32[512]{0:T(512)S(1)} %convert_element_type.64, f32[4096]{0:T(1024)S(1)} %fusion.40, ...), kind=kLoop, calls=%fused_computation.125 | loop fusion | flops 31453184 | bytes 37836800 | tf_op jit(solution)/shard_map/transpose(jvp())/reduce_sum | solution.py:13
  244.8 3.3 copy-done
  248.1 11.5 %fusion.24 = f32[512,1536]{1,0:T(8,128)} fusion(bf16[4095,512]{1,0:T(8,128)(2,1)} %slice.41, bf16[4096,1024]{1,0:T(8,128)(2,1)} %reshape.198, f32[4096,512]{0,1:T(8,128)S(1)} %get-tuple-element.83, f32[4096]{0:T(1024)S(1)} %negate_multiply_fusion.3), kind=kOutput, calls=%fused_computation.67 | convolution fusion | flops 6484393984 | bytes 24132608 | tf_op jit(solution)/shard_map/dot_general | solution.py:150
  259.7 14.6 %fusion.29 = f32[4096,1536]{1,0:T(8,128)} fusion(bf16[512,1536]{1,0:T(8,128)(2,1)} %all-gather.3.cloned.1.call-done, f32[4096,512]{0,1:T(8,128)} %copy-done, f32[4096]{0:T(1024)S(1)} %negate_multiply_fusion.3), kind=kOutput, calls=%fused_computation.71 | convolution fusion | flops 6446645248 | bytes 35143680 | tf_op jit(solution)/shard_map/dot_general | solution.py:75
  274.3 4.4 slice.43
  278.6 12.5 %pad_add_fusion = f32[4096,1024]{1,0:T(8,128)} fusion(f32[4095,512]{1,0:T(8,128)S(1)} %slice.43, f32[4096,1536]{1,0:T(8,128)} %fusion.29), kind=kLoop, calls=%fused_computation.6 | loop fusion | flops 4194304 | bytes 41940992 | tf_op jit(solution)/shard_map/add | solution.py:80
  291.1 18.3 %reshape.199 = f32[8192,512]{1,0:T(8,128)} reshape(f32[4096,1024]{1,0:T(8,128)} %pad_add_fusion) | data formatting | bytes 33554432 | tf_op jit(solution)/shard_map/reshape | solution.py:82
  309.4 17.5 %copy.53 = f32[8192,512]{0,1:T(8,128)} copy(f32[8192,512]{1,0:T(8,128)} %reshape.199) | data formatting | bytes 33554432 | tf_op jit(solution)/shard_map/reshape | solution.py:82
  326.9 29.7 %multiply_reduce_fusion = (f32[512]{0:T(512)S(1)}, f32[8192]{0:T(1024)S(1)}, f32[512]{0:T(512)S(1)}, f32[8192,512]{0,1:T(8,128)}) fusion(f32[8192]{0:T(1024)S(1)} %fusion.39, f32[8192]{0:T(1024)S(1)} %broadcast_multiply_fusion, f32[8192,512]{0,1:T(8,128)} %get-tuple-element.98, f32[512]{0:T(512)S(1)} %convert_element_type.58, ...), kind=kLoop, calls=%fused_computation.7 | loop fusion | flops 104848384 | bytes 67250176 | tf_op jit(solution)/shard_map/transpose(jvp())/reduce_sum | solution.py:15
  356.7 13.1 %fusion.55 = (f32[8192]{0:T(1024)S(1)}, f32[8192,512]{0,1:T(8,128)}) fusion(f32[8192]{0:T(1024)S(1)} %multiply_multiply_fusion.10, f32[8192]{0:T(1024)S(1)} %broadcast_multiply_fusion, f32[8192,512]{0,1:T(8,128)S(1)} %bitcast.42, f32[512]{0:T(512)S(1)} %convert_element_type.58, f32[8192]{0:T(1024)S(1)} %fusion.39, f32[8192,512]{0,1:T(8,128)} %get-tuple-element.81, ...), kind=kLoop, calls=%fused_computation.124 | loop fusion | flops 33546240 | bytes 50466816 | tf_op jit(solution)/shard_map/transpose(jvp())/reduce_sum | solution.py:13
  369.9 8.8 %fusion.9 = f32[512,10]{1,0:T(8,128)} fusion(f32[8192,512]{0,1:T(8,128)} %get-tuple-element.80, f32[8192]{0:T(1024)S(1)} %negate_multiply_fusion.2, bf16[8191,5]{0,1:T(8,128)(2,1)S(1)} %copy-done.5, bf16[8192,5]{0,1:T(8,128)(2,1)S(1)} %copy-done.3), kind=kOutput, calls=%fused_computation.34 | convolution fusion | flops 92766208 | bytes 16994294
  378.7 7.0 %add_reduce_fusion = f32[512]{0:T(512)S(1)} fusion(f32[8192,512]{0,1:T(8,128)} %get-tuple-element.80, f32[8192]{0:T(1024)S(1)} %negate_multiply_fusion.2), kind=kLoop, calls=%fused_computation.26 | loop fusion | flops 8388096 | bytes 16812032 | tf_op jit(solution)/shard_map/reduce_sum | solution.py:84
  385.8 4.1 add_reduce_fusion.2
  389.8 6.4 %copy.54 = bf16[1,4096,512]{2,1,0:T(8,128)(2,1)} copy(bf16[1,4096,512]{1,2,0:T(8,128)(2,1)} %get-tuple-element.88) | data formatting | bytes 8388608
  396.3 58.5 %all-reduce.16 = (f32[512]{0:T(512)S(1)}, f32[512]{0:T(512)S(1)}, f32[512]{0:T(512)S(1)}, f32[512]{0:T(512)S(1)}, f32[512]{0:T(512)S(1)}, /*index=5*/f32[512]{0:T(512)S(1)}) all-reduce(f32[512]{0:T(512)S(1)} %add_reduce_fusion, f32[512]{0:T(512)S(1)} %get-tuple-element.54, ...), channel_id=3, replica_groups=mesh['dp'=8,'fsdp'=16] {'fsdp'}, use_global_device_ids=true, to_apply=%region_14.15.clone | all-reduce | flops 3072 | bytes 24576
  455.2 5.4 %reduce-scatter.7.cloned.1.call-done = f32[32,10]{1,0:T(8,128)} async-done(((f32[512,10]{1,0:T(8,128)}), f32[32,10]{1,0:T(8,128)}) %reduce-scatter.7.cloned.1.call-update) | async-done | bytes 1296
  461.4 41.0 %all-reduce.17 = (f32[32,10]{0,1:T(8,128)}, f32[32]{0:T(128)}, f32[32]{0:T(128)}, f32[32]{0:T(128)}, f32[32]{0:T(128)}, /*index=5*/f32[32]{0:T(128)}, f32[32]{0:T(128)}) all-reduce(f32[32,10]{0,1:T(8,128)S(1)} %copy.56, f32[32]{0:T(128)S(1)} %dynamic-slice.7, f32[32]{0:T(128)S(1)} %dynamic-slice.9, ...), channel_id=1, replica_groups=mesh['dp'=8,'fsdp'=16] {'dp'}, use_global_device_ids=true, to_apply=%region_12.13 | all-reduce | flops 512 | bytes 4096 | tf_op jit(solution)/shard_map/psum | solution.py:166
  502.3 19.0 %all-reduce.21.cloned.1.call-done = f32[32,1536]{1,0:T(8,128)} async-done(((f32[32,1536]{1,0:T(8,128)}), f32[32,1536]{1,0:T(8,128)}) %all-reduce.21.cloned.1.call-update) | async-done | bytes 196624 | tf_op jit(solution)/shard_map/psum | solution.py:166
  (114 shorter events, 17.9 us)
Async XLA Ops:
  7.2 34.6 %copy-start.9 = (u32[128]{0:T(128)S(1)}, u32[128]{0:T(128)}, u32[]{:S(2)}) copy-start(u32[128]{0:T(128)} %constant.32) | copy-start | bytes 1540
  7.2 34.5 %copy-start.10 = (s32[1,128]{1,0:T(1,128)S(1)}, s32[1,128]{1,0:T(1,128)}, u32[]{:S(2)}) copy-start(s32[1,128]{1,0:T(1,128)} %param.14) | copy-start | bytes 1540
  7.2 35.8 %copy-start.11 = (bf16[32]{0:T(256)(128)(2,1)S(1)}, bf16[32]{0:T(256)(128)(2,1)}, u32[]{:S(2)}) copy-start(bf16[32]{0:T(256)(128)(2,1)} %param.16) | copy-start | bytes 196
  7.2 36.0 %copy-start.12 = (bf16[32]{0:T(256)(128)(2,1)S(1)}, bf16[32]{0:T(256)(128)(2,1)}, u32[]{:S(2)}) copy-start(bf16[32]{0:T(256)(128)(2,1)} %param.17) | copy-start | bytes 196
  7.2 36.3 %copy-start.13 = (bf16[32]{0:T(256)(128)(2,1)S(1)}, bf16[32]{0:T(256)(128)(2,1)}, u32[]{:S(2)}) copy-start(bf16[32]{0:T(256)(128)(2,1)} %param.18) | copy-start | bytes 196
  7.2 36.5 %copy-start.14 = (bf16[32]{0:T(256)(128)(2,1)S(1)}, bf16[32]{0:T(256)(128)(2,1)}, u32[]{:S(2)}) copy-start(bf16[32]{0:T(256)(128)(2,1)} %param.21) | copy-start | bytes 196
  7.2 36.8 %copy-start.15 = (bf16[32]{0:T(256)(128)(2,1)S(1)}, bf16[32]{0:T(256)(128)(2,1)}, u32[]{:S(2)}) copy-start(bf16[32]{0:T(256)(128)(2,1)} %param.22) | copy-start | bytes 196
  7.3 37.0 %copy-start.16 = (bf16[32]{0:T(256)(128)(2,1)S(1)}, bf16[32]{0:T(256)(128)(2,1)}, u32[]{:S(2)}) copy-start(bf16[32]{0:T(256)(128)(2,1)} %param.20) | copy-start | bytes 196
  7.3 72.5 %copy-start.8 = (bf16[32,10]{0,1:T(8,128)(2,1)S(1)}, bf16[32,10]{0,1:T(8,128)(2,1)}, u32[]{:S(2)}) copy-start(bf16[32,10]{0,1:T(8,128)(2,1)} %param.15) | copy-start | bytes 1924
  7.3 188.0 %all-gather.3.cloned.1.call-start = ((), (), s32[]{:S(2)}) async-start(), calls=%async_computation.2 | async-start | bytes 1671168 | tf_op jit(solution)/shard_map/all_gather | solution.py:141
  8.0 377.7 %reduce-scatter.5.cloned.1.call-start = ((), (), s32[]{:S(2)}) async-start(), calls=%async_computation.3 | async-start | bytes 3342336 | tf_op jit(solution)/shard_map/reduce_scatter | solution.py:149
  39.8 65.8 %copy-start.2 = (bf16[8192,5]{0,1:T(8,128)(2,1)}, bf16[8192,5]{0,1:T(8,128)(2,1)S(1)}, u32[]{:S(2)}) copy-start(bf16[8192,5]{0,1:T(8,128)(2,1)S(1)} %copy.47) | copy-start | bytes 245764
  97.5 8.1 %copy-start.4 = (bf16[8191,5]{0,1:T(8,128)(2,1)}, bf16[8191,5]{0,1:T(8,128)(2,1)S(1)}, u32[]{:S(2)}) copy-start(bf16[8191,5]{0,1:T(8,128)(2,1)S(1)} %copy.57) | copy-start | bytes 245734
  114.2 43.2 %copy-start.6 = (f32[8192]{0:T(1024)}, f32[8192]{0:T(1024)S(1)}, u32[]{:S(2)}) copy-start(f32[8192]{0:T(1024)S(1)} %multiply_reduce_fusion.2) | copy-start | bytes 98308
  205.2 2.2 copy-start.1
  244.8 3.3 copy-start
  259.7 200.9 %reduce-scatter.7.cloned.1.call-start = ((), (), s32[]{:S(2)}) async-start(), calls=%async_computation.5 | async-start | bytes 278528
  326.9 29.8 %slice-start = ((s8[16777216]{0:T(1024)(128)(4,1)}), s8[4194304]{0:T(1024)(128)(4,1)S(1)}, s32[]{:S(2)}) async-start(s8[16777216]{0:T(1024)(128)(4,1)} %bitcast.41), calls=%async_computation.6 | async-start | bytes 8388608
  326.9 29.7 %copy-start.7 = (f32[8192]{0:T(1024)S(1)}, f32[8192]{0:T(1024)}, u32[]{:S(2)}) copy-start(f32[8192]{0:T(1024)} %copy-done.6) | copy-start | bytes 98308
  326.9 29.8 %slice-start.1 = ((s8[16777216]{0:T(1024)(128)(4,1)}), s8[4194304]{0:T(1024)(128)(4,1)S(1)}, s32[]{:S(2)}) async-start(s8[16777216]{0:T(1024)(128)(4,1)} %bitcast.41), calls=%async_computation.7 | async-start | bytes 8388608
  326.9 29.8 %slice-start.2 = ((s8[16777216]{0:T(1024)(128)(4,1)}), s8[4194304]{0:T(1024)(128)(4,1)S(1)}, s32[]{:S(2)}) async-start(s8[16777216]{0:T(1024)(128)(4,1)} %bitcast.41), calls=%async_computation.8 | async-start | bytes 8388608
  326.9 29.8 %slice-start.3 = ((s8[16777216]{0:T(1024)(128)(4,1)}), s8[4194304]{0:T(1024)(128)(4,1)S(1)}, s32[]{:S(2)}) async-start(s8[16777216]{0:T(1024)(128)(4,1)} %bitcast.41), calls=%async_computation.9 | async-start | bytes 8388608
  356.7 13.2 %copy-start.3 = (bf16[8192,5]{0,1:T(8,128)(2,1)S(1)}, bf16[8192,5]{0,1:T(8,128)(2,1)}, u32[]{:S(2)}) copy-start(bf16[8192,5]{0,1:T(8,128)(2,1)} %copy-done.2) | copy-start | bytes 245764
  356.7 13.2 %copy-start.5 = (bf16[8191,5]{0,1:T(8,128)(2,1)S(1)}, bf16[8191,5]{0,1:T(8,128)(2,1)}, u32[]{:S(2)}) copy-start(bf16[8191,5]{0,1:T(8,128)(2,1)} %copy-done.4) | copy-start | bytes 245734
  378.7 142.7 %all-reduce.21.cloned.1.call-start = ((), (), s32[]{:S(2)}) async-start(), calls=%async_computation.4 | async-start | bytes 393216 | tf_op jit(solution)/shard_map/psum | solution.py:166
Sparse Core Ops, SparseCore 0:
  10.2 46.3 all-gather.2
  259.8 85.5 reduce-scatter.4
  378.8 81.7 reduce-scatter.6
  462.8 58.4 all-reduce.20
where the time goes:
time: 539 us; the launch traced here: 530 us
  other arithmetic  166 us (31%)
  blocking collectives  165 us (31%)
  local copies, waits for them, and re-layouts  105 us (19%)
  matrix products  52.8 us (10%)
  waiting for transfers between devices  25.2 us (5%)
  between operations  15.8 us (3%)
    unnamed x2, blocking collectives  93.4 us
    reduce_sum x2, other arithmetic, norm_act(): scaled = centred * lax.rsqrt(spread + epsilon) * scale_by + shift_by  57.2 us
    convert_element_type x1, other arithmetic, local_pass(): hidden = post_first.astype(jnp.bfloat16)  43.1 us
    psum x1, blocking collectives, local(): lax.psum((second_part, summed[0], summed[1], summed[2], summed[3], summed...  41 us
    reshape x2, local copies, waits for them, and re-layouts, local_pass(): grad_hidden = (grad_columns[:, :2 * channels] + jnp.concatenate([shifted,...  35.8 us
    unnamed x67, local copies, waits for them, and re-layouts  24.1 us
    reduce_sum x2, other arithmetic, norm_act(): centred = pre_act - average  23.1 us
    psum x1, waiting for transfers between devices, local(): lax.psum((second_part, summed[0], summed[1], summed[2], summed[3], summed...  19 us
  transfers between devices with their start and end apart: 4, of which 2 were waited for; matrix products, arithmetic and copies ran while one was open for 49% of the time, Pallas kernels for 0%

commit v1 on v0

v1 whole, which is shorter than its diff:
```python
import jax
import jax.numpy as jnp
import numpy as np
from jax import lax
from jax.experimental import pallas as pl
from jax.experimental.pallas import tpu as pltpu
from jax.sharding import PartitionSpec as P

MESH = pl.DeviceIdType.MESH
F32, BF16, I32 = jnp.float32, jnp.bfloat16, jnp.int32
EXACT = lax.Precision.HIGHEST
CH, FRAMES, ROWS, TILE, STEPS = 512, 128, 4096, 256, 16
DP, FS = 8, 16
SHARD, SLOT, TAPS = 32, 16, 10
EPS = 1e-05
HALF = 0.7071067811865476
EXP_BY = -1.4426950408889634
EXP_PLUS = -0.32574806470870245


def mm(a, b, dims, precision=None):
    return lax.dot_general(
        a, b, (dims, ((), ())), precision=precision, preferred_element_type=F32
    )


def iota(shape, axis):
    return lax.broadcasted_iota(I32, shape, axis)


def patch_tables():
    lane = np.arange(384)
    at = np.arange(TILE + 16) % 32
    mask = (lane[None, :] // TAPS == at[:, None]) & (lane < 320)[None, :]
    mask |= (lane == 320)[None, :]
    mask |= (lane == 321)[None, :] & (at != 31)[:, None]
    mask |= (lane == 322)[None, :] & (at == 31)[:, None]
    pick = np.zeros((384, 384), np.float32)
    for group in (0, 16, 32):
        for sample in range(320):
            tap = sample % TAPS
            pick[sample, group + tap] = 1
            if tap >= 5:
                pick[sample, 128 + group + tap - 5] = 1
            else:
                pick[sample, 256 + group + tap + 5] = 1
    for lane_out in (48, 49):
        pick[320, lane_out] = 1
        pick[321, 128 + lane_out] = 1
        pick[322, 128 + lane_out] = 1
    return jnp.asarray(mask, BF16), jnp.asarray(pick, BF16)


def greet(dp, fs):
    barrier = pltpu.get_barrier_semaphore()
    for k in range(1, DP):
        pl.semaphore_signal(barrier, inc=1, device_id=(lax.rem(dp + k, DP), fs), device_id_type=MESH)
    for k in range(1, FS):
        pl.semaphore_signal(barrier, inc=1, device_id=(dp, lax.rem(fs + k, FS)), device_id_type=MESH)
    pl.semaphore_wait(barrier, DP + FS - 2)


def send(src, dst, send_sem, recv_sem, device):
    return pltpu.make_async_remote_copy(
        src_ref=src, dst_ref=dst, send_sem=send_sem, recv_sem=recv_sem,
        device_id=device, device_id_type=MESH,
    )


def centred_weights(small):
    centred = small - jnp.mean(small, axis=1, keepdims=True)
    return jnp.where(iota((16, CH), 0) <= TAPS, centred, 0.0)


def split(value):
    high = value.astype(BF16).astype(F32)
    return high, value - high


def first_kernel(
    list_ref, seg_ref, wave_ref, weight_ref, vec_ref, second_ref, mask_ref, pick_ref,
    he_ref, ho_ref, de_ref, do_ref, le_ref, lo_ref, small_ref, second_out,
    slots, heard, small_own, smalls, second_all, frames, rhs, quad,
    a2a_s, a2a_r, sm_s, sm_r, w_s, w_r, fw_s, fw_r, out_sem,
):
    step = pl.program_id(0)
    dp, fs = lax.axis_index("dp"), lax.axis_index("fsdp")
    core = lax.rem(dp, 2)
    sibling = dp + 1 - 2 * core
    half = pl.ds(pl.multiple_of(core * 768, 128), 768)

    def a2a_copy(k):
        target = lax.rem(dp + k, DP)
        return send(
            slots.at[pl.ds(pl.multiple_of(target * SLOT, SLOT), SLOT)],
            heard.at[pl.ds(pl.multiple_of(dp * SLOT, SLOT), SLOT)],
            a2a_s.at[k], a2a_r.at[k], (target, fs),
        )

    def small_copy(k):
        return send(small_own, smalls.at[fs], sm_s.at[k], sm_r.at[k], (dp, lax.rem(fs + k, FS)))

    def second_copy(k):
        rows = pl.ds(pl.multiple_of(fs * SHARD, SHARD), SHARD)
        return send(
            second_ref.at[:, half], second_all.at[rows, half],
            w_s.at[k], w_r.at[k], (dp, lax.rem(fs + k, FS)),
        )

    def forward_copy(k):
        rows = pl.ds(pl.multiple_of(lax.rem(fs + FS - k, FS) * SHARD, SHARD), SHARD)
        piece = second_all.at[rows, half]
        return send(piece, piece, fw_s.at[k], fw_r.at[k], (sibling, fs))

    @pl.when(step == 0)
    def _():
        table = list_ref[...].astype(F32)
        eye = iota((128, 128), 0) == iota((128, 128), 1)

        def row(i):
            return jnp.broadcast_to(table[i : i + 1], (128, 128))

        def col(value):
            return jnp.sum(jnp.where(eye, value, 0.0), axis=1, keepdims=True)

        source, owner, place, length = row(0), row(1), row(2), row(3)
        source_c, owner_c, length_c = col(source), col(owner), col(length)
        earlier = (iota((128, 128), 0) < iota((128, 128), 1)) & (source_c == source)
        read_at = jnp.sum(jnp.where(earlier, length_c, 0.0), axis=0, keepdims=True)
        slot_at = jnp.sum(
            jnp.where(earlier & (owner_c == owner), length_c, 0.0), axis=0, keepdims=True
        )
        read_at = jnp.broadcast_to(read_at, (128, 128))
        slot_at = jnp.broadcast_to(slot_at, (128, 128))
        row_at = iota((128, 128), 0)
        lane_f = iota((128, 128), 1).astype(F32)
        group = (row_at // SLOT).astype(F32)
        inner = (row_at % SLOT).astype(F32)
        me = dp.astype(F32)
        entry = (
            (owner == group) & (source == me)
            & (slot_at <= inner) & (inner < slot_at + length)
        )
        frame = jnp.sum(jnp.where(entry, read_at + inner - slot_at + 1.0, 0.0), axis=1, keepdims=True)
        pack = jnp.where(lane_f + 1.0 == frame, 1.0, 0.0).astype(BF16)
        slots[...] = mm(pack, wave_ref[0], ((1,), (0,))).astype(BF16)

        place_lanes = jnp.where(
            iota((SHARD, 128), 1) == iota((SHARD, 128), 0) + lax.rem(fs, 4) * SHARD, 1.0, 0.0
        ).astype(BF16)
        quad[0:TAPS, 0:128] = mm(weight_ref[...], place_lanes, ((0,), (0,)))
        quad[TAPS:16, 0:128] = mm(vec_ref[...], place_lanes, ((1,), (0,)))
        small_own[...] = quad[0:16, 0:128].astype(BF16)

        greet(dp, fs)
        for k in range(1, DP):
            a2a_copy(k).start()
        for k in range(1, FS):
            small_copy(k).start()
        for k in range(1, FS):
            second_copy(k).start()

        mine = pl.ds(pl.multiple_of(dp * SLOT, SLOT), SLOT)
        heard[mine] = slots[mine]
        smalls[pl.ds(fs, 1)] = small_own[...][None]
        second_all[pl.ds(pl.multiple_of(fs * SHARD, SHARD), SHARD)] = second_ref[...]

        position = row_at.astype(F32)
        entry = (owner == me) & (position >= place) & (position < place + length)
        origin = jnp.sum(
            jnp.where(entry, source * SLOT + slot_at + position - place + 1.0, 0.0),
            axis=1, keepdims=True,
        )
        unpack = jnp.where(lane_f + 1.0 == origin, 1.0, 0.0).astype(BF16)
        seg = jnp.broadcast_to(seg_ref[...].astype(F32), (128, 128))
        following = jnp.where(iota((128, 128), 1) == 127, -1.0, pltpu.roll(seg, 127, 1))
        inside = jnp.where(seg >= 0, 1.0, 0.0)
        inside_c = col(inside)
        kept_c = col(jnp.where(following != seg, 0.0, inside))
        lane = iota((128, 128), 1)
        flags = jnp.where(
            (lane == 64) | (lane == 65), inside_c, jnp.where(lane == 66, kept_c, 0.0)
        )

        for k in range(1, FS):
            small_copy(k).wait_recv()
        parts = []
        for g in range(4):
            total = smalls[4 * g].astype(F32)
            for q in range(1, 4):
                total = total + smalls[4 * g + q].astype(F32)
            parts.append(total)
        small = jnp.concatenate(parts, axis=1)
        small_ref[...] = small
        centred = centred_weights(small)
        high, low = split(centred * small[11:12] * HALF)
        shift_high, shift_low = split(small[12:13] * HALF)
        r16 = iota((16, CH), 0)
        shifts = jnp.where(r16 == 0, shift_high, jnp.where(r16 == 1, shift_low, 0.0))
        rhs[...] = jnp.concatenate(
            [high, low, high, shifts, jnp.zeros((64, CH), F32)], axis=0
        ).astype(BF16)
        wide = jnp.concatenate([centred, jnp.zeros((112, CH), F32)], axis=0)
        gram = mm(centred, wide, ((1,), (1,)), EXACT) * (1.0 / CH)
        gram_a, rest = split(gram)
        gram_b, gram_c = split(rest)
        quad[:, 0:128] = jnp.concatenate(
            [gram_a, gram_b, gram_c, jnp.zeros((80, 128), F32)], axis=0
        )
        quad[:, 128:256] = jnp.where(row_at == 48, 1.0, 0.0)

        for k in range(1, DP):
            a2a_copy(k).wait_recv()
        packed = mm(unpack, heard[...], ((1,), (0,)))
        frames[0:128, 256:384] = flags
        frames[0:128, 0:320] = packed
        frames[128:144, :] = jnp.zeros((16, 384), F32)

    few = frames[pl.ds(pl.multiple_of(step * 8, 8), 16)].astype(BF16)
    spread = iota((TILE + 16, 16), 0)
    start = iota((TILE + 16, 16), 1) * 32
    repeat = jnp.where((spread >= start) & (spread < start + 32), 1.0, 0.0).astype(BF16)
    wide = mm(repeat, few, ((1,), (0,))).astype(BF16) * mask_ref[...]
    taken = mm(wide, pick_ref[...], ((1,), (0,)))
    even = taken[:TILE, 0:128]
    odd = taken[:TILE, 128:256] + pltpu.roll(taken[:, 256:384], TILE + 15, 0)[:TILE]
    lane1 = iota((1, 128), 1)
    bias_lane = jnp.where((lane1 == 10) | (lane1 == 26) | (lane1 == 42), 1.0, 0.0)
    patch = jnp.concatenate([even, odd], axis=0) + bias_lane
    form = mm(patch.astype(BF16), quad[...].astype(BF16), ((1,), (0,)))
    var = jnp.sum(form[:, 0:128] * patch, axis=1, keepdims=True)
    scale = lax.rsqrt(jnp.maximum(var, 0.0) + EPS) * form[:, 128:256]
    scaled = patch * scale
    high, low = split(scaled)
    lane_t = iota((2 * TILE, 128), 1)
    left = jnp.where(lane_t < 32, high, jnp.where(lane_t < 48, low, patch)).astype(BF16)
    for part, (h_ref, d_ref, l_ref) in enumerate(((he_ref, de_ref, le_ref), (ho_ref, do_ref, lo_ref))):
        piece = left[part * TILE : (part + 1) * TILE]
        l_ref[...] = piece
        u = mm(piece, rhs[...], ((1,), (0,)))
        phi = HALF * lax.erf(u) + HALF
        h_ref[...] = (u * phi).astype(BF16)
        bell = jnp.exp2(u * u * EXP_BY + EXP_PLUS)
        d_ref[...] = (phi + u * bell).astype(BF16)

    @pl.when(step > 0)
    def _():
        second_copy(step).wait_recv()
        forward_copy(step).start()

    @pl.when(step == STEPS - 1)
    def _():
        for k in range(1, FS):
            forward_copy(k).wait_recv()
        out = pltpu.make_async_copy(second_all, second_out, out_sem)
        out.start()
        for k in range(1, DP):
            a2a_copy(k).wait_send()
        for k in range(1, FS):
            small_copy(k).wait_send()
            second_copy(k).wait_send()
            forward_copy(k).wait_send()
        out.wait()


def second_kernel(
    he_ref, ho_ref, halo_ref, lo_ref, cot_ref, weight_ref, small_ref,
    feat_ref, g_ref, gs_ref, sums_ref, carry,
):
    step = pl.program_id(0)

    @pl.when(step == 0)
    def _():
        sums_ref[...] = jnp.zeros_like(sums_ref)
        carry[...] = jnp.zeros_like(carry)

    bias = small_ref[13:14]
    gain = small_ref[14:15]
    shift = small_ref[15:16]
    keep = lo_ref[...].astype(F32)[:, 48:49]
    even = he_ref[...]
    pre = mm(even, weight_ref[:, 0:CH], ((1,), (1,))) + mm(ho_ref[...], weight_ref[:, CH : 2 * CH], ((1,), (1,)))
    halo = halo_ref[...]
    halo = jnp.where(step == STEPS - 1, jnp.zeros_like(halo), halo)
    third = mm(jnp.concatenate([even, halo], axis=0), weight_ref[:, 2 * CH :], ((1,), (1,)))
    pre = pre + pltpu.roll(third, TILE + 15, 0)[:TILE] + bias
    centred = pre - jnp.mean(pre, axis=1, keepdims=True)
    var = jnp.mean(centred * centred, axis=1, keepdims=True)
    scale = lax.rsqrt(var + EPS)
    norm = centred * scale
    u = norm * (gain * HALF) + shift * HALF
    phi = HALF * lax.erf(u) + HALF
    feat_ref[0] = (u * phi * keep).astype(BF16)
    bell = jnp.exp2(u * u * EXP_BY + EXP_PLUS)
    slope = phi + u * bell
    dnorm = cot_ref[0].astype(F32) * (keep * HALF) * slope * gain
    prod = dnorm * norm
    mean_a = jnp.mean(dnorm, axis=1, keepdims=True)
    mean_b = jnp.mean(prod, axis=1, keepdims=True)
    dpre = (dnorm - mean_a - norm * mean_b) * scale
    sums_ref[0:8] += jnp.sum(dpre.reshape(TILE // 8, 8, CH), axis=0)
    sums_ref[8:16] += jnp.sum(prod.reshape(TILE // 8, 8, CH), axis=0)
    sums_ref[16:24] += jnp.sum(dnorm.reshape(TILE // 8, 8, CH), axis=0)
    g_ref[...] = dpre.astype(BF16)
    rolled = pltpu.roll(dpre, 1, 0)
    rolled = jnp.where(iota((TILE, CH), 0) == 0, carry[0:1], rolled)
    gs_ref[...] = rolled.astype(BF16)
    carry[0:1] = dpre[TILE - 1 : TILE]


def third_kernel(
    he_in, ho_in, g_in, gs_in, de_in, do_in, le_in, lo_in, weight_ref, small_ref, sums_ref,
    second_grad, first_grad, vec_b, vec_g, vec_s, vec_b2, vec_g2, vec_s2,
    he, ho, g1, gs, de, do, le, lo, total, half_bf, pair_in, pair_sum, y_in, y_sum, f_in, f_sum,
    gathered, wz, t_acc, r_acc, small_own, small_in, small_sum, small_dp,
    load, p_s, p_r, y_s, y_r, f_s, f_r, d_s, d_r, s_s, s_r, e_s, e_r,
):
    dp, fs = lax.axis_index("dp"), lax.axis_index("fsdp")
    core = lax.rem(dp, 2)
    yy = dp // 2
    sibling = dp + 1 - 2 * core
    quarter = pl.ds(pl.multiple_of(yy * 384, 128), 384)
    parts = ROWS // 4

    def chunk(k):
        return pl.ds(k * parts, parts)

    def chunk_loads(k):
        return [
            pltpu.make_async_copy(src.at[chunk(k)], dst.at[chunk(k)], load.at[i, k])
            for i, (src, dst) in enumerate(((g_in, g1), (gs_in, gs), (he_in, he), (ho_in, ho)))
        ]

    late = [
        pltpu.make_async_copy(src, dst, load.at[4 + i, 0])
        for i, (src, dst) in enumerate(((de_in, de), (do_in, do), (le_in, le), (lo_in, lo)))
    ]
    for k in range(4):
        for copy in chunk_loads(k):
            copy.start()
    for copy in late:
        copy.start()
    greet(dp, fs)

    def pair_copy(m):
        four = pl.ds(m * 4, 4)
        return send(half_bf.at[four, 1 - core], pair_in.at[four], p_s.at[m], p_r.at[m], (sibling, fs))

    def y_copy(k):
        target = lax.rem(yy + k, 4)
        return send(
            pair_sum.at[:, :, pl.ds(pl.multiple_of(target * 384, 128), 384)], y_in.at[k],
            y_s.at[k], y_r.at[k], (target * 2 + core, fs),
        )

    def f_copy(k):
        target = lax.rem(fs + k, FS)
        return send(y_sum.at[target], f_in.at[k], f_s.at[k], f_r.at[k], (dp, target))

    def d_copy(k):
        rows = pl.ds(pl.multiple_of(core * 16, 16), 16)
        return send(f_sum, gathered.at[rows, quarter], d_s.at[k], d_r.at[k], (lax.rem(dp + k, DP), fs))

    def s_copy(k):
        target = lax.rem(fs + k, FS)
        return send(small_own.at[target // 4], small_in.at[k], s_s.at[k], s_r.at[k], (dp, target))

    def e_copy(k):
        return send(small_sum, small_dp.at[k], e_s.at[k], e_r.at[k], (lax.rem(dp + k, DP), fs))

    small = small_ref[...]
    centred = centred_weights(small)
    gain = small[11:12]
    high, low = split(centred * gain)
    r16 = iota((16, CH), 0)
    wz[...] = jnp.concatenate(
        [high, low, high, jnp.where(r16 == 0, gain, 0.0), jnp.zeros((64, CH), F32)], axis=0
    ).astype(BF16)
    t_acc[...] = jnp.zeros_like(t_acc)
    r_acc[...] = jnp.zeros_like(r_acc)

    for k in range(4):
        for copy in chunk_loads(k):
            copy.wait()

        def block(m, _, k=k):
            cols = pl.ds(pl.multiple_of(m * 128, 128), 128)
            rows = chunk(k)
            g_part, gs_part = g1[rows, cols], gs[rows, cols]
            for c, (left, right) in enumerate(((g_part, he), (g_part, ho), (gs_part, he))):
                lanes = pl.ds(c * CH, CH)
                value = mm(left, right[rows], ((0,), (0,)))
                if k > 0:
                    value = value + total[cols, lanes]
                if k < 3:
                    total[cols, lanes] = value
                else:
                    half_bf[pl.ds(m * 4, 4), :, :, lanes] = value.astype(BF16).reshape(4, 2, 16, CH)
            if k == 3:
                pair_copy(m).start()
            return 0

        lax.fori_loop(0, 4, block, 0)
    for copy in late:
        copy.wait()

    def tile(i, _):
        rows = pl.ds(pl.multiple_of(i * TILE, TILE), TILE)
        g_tile = g1[rows]
        d_even = mm(g_tile, weight_ref[:, 0:CH], ((1,), (0,))) + mm(gs[rows], weight_ref[:, 2 * CH :], ((1,), (0,)))
        d_odd = mm(g_tile, weight_ref[:, CH : 2 * CH], ((1,), (0,)))
        lane = iota((TILE, 128), 1)
        for d_hidden, slope, lhs in ((d_even, de, le), (d_odd, do, lo)):
            ds = (d_hidden * slope[rows].astype(F32)).astype(BF16)
            left = lhs[rows]
            left_f = left.astype(F32)
            z = mm(ds, wz[...], ((1,), (1,)))
            inner = jnp.where(lane < 48, z * left_f, 0.0)
            corr = jnp.sum(inner, axis=1, keepdims=True)
            y = jnp.where(lane < 48, corr * left_f, z).astype(BF16)
            t_acc[...] += mm(left, ds, ((0,), (0,)))
            r_acc[...] += mm(y, left, ((0,), (0,)))

        @pl.when(i == 2)
        def _():
            for m in range(4):
                pair_copy(m).wait_recv()
                four = pl.ds(m * 4, 4)
                pair_sum[four] = (
                    half_bf[four, core].astype(F32) + pair_in[four].astype(F32)
                ).astype(BF16)
            for k in range(1, 4):
                y_copy(k).start()

        @pl.when(i == 9)
        def _():
            value = pair_sum[:, :, quarter].astype(F32)
            for k in range(1, 4):
                y_copy(k).wait_recv()
                value = value + y_in[k].astype(F32)
            y_sum[...] = value
            for k in range(1, FS):
                f_copy(k).start()

        @pl.when(i == 13)
        def _():
            value = y_sum[fs]
            for k in range(1, FS):
                f_copy(k).wait_recv()
                value = value + f_in[k]
            f_sum[...] = value
            for k in range(1, DP):
                d_copy(k).start()

        return 0

    lax.fori_loop(0, STEPS, tile, 0)

    t_core = t_acc[0:16] + t_acc[32:48]
    r_rows = jnp.concatenate(
        [r_acc[0:16] + r_acc[32:48], jnp.where(iota((8, 128), 0) == 0, r_acc[48:56], 0.0)], axis=0
    )
    r_rows = r_rows + pltpu.roll(r_rows, 96, 1)
    right = jnp.concatenate([centred, jnp.where(iota((8, CH), 0) == 0, 1.0, 0.0)], axis=0)
    corr = mm(r_rows, right, ((0,), (0,)), EXACT)[0:16] * (1.0 / CH)
    grad = (gain * t_core - corr) * HALF
    gain_grad = jnp.sum(centred * t_core, axis=0, keepdims=True) * HALF
    shift_grad = t_acc[48:49] * HALF
    sums = sums_ref[...]
    inv = 1.0 / small[14:15]
    grad = jnp.where(r16 == 11, gain_grad, grad)
    grad = jnp.where(r16 == 12, shift_grad, grad)
    grad = jnp.where(r16 == 13, jnp.sum(sums[0:8], axis=0, keepdims=True), grad)
    grad = jnp.where(r16 == 14, jnp.sum(sums[8:16], axis=0, keepdims=True) * inv, grad)
    grad = jnp.where(r16 == 15, jnp.sum(sums[16:24], axis=0, keepdims=True) * inv, grad)
    for q in range(4):
        small_own[q] = grad[:, q * 128 : (q + 1) * 128]
    for k in range(1, FS):
        s_copy(k).start()

    rows16 = pl.ds(pl.multiple_of(core * 16, 16), 16)
    gathered[rows16, quarter] = f_sum[...]
    for k in range(1, DP):
        d_copy(k).wait_recv()
    second_grad[...] = gathered[...]

    value = small_own[fs // 4]
    for k in range(1, FS):
        s_copy(k).wait_recv()
        value = value + small_in[k]
    small_sum[...] = value
    for k in range(1, DP):
        e_copy(k).start()
    for m in range(4):
        pair_copy(m).wait_send()
    for k in range(1, 4):
        y_copy(k).wait_send()
    for k in range(1, FS):
        f_copy(k).wait_send()
        s_copy(k).wait_send()
    for k in range(1, DP):
        d_copy(k).wait_send()
        e_copy(k).wait_recv()
        value = value + small_dp[k]
    for k in range(1, DP):
        e_copy(k).wait_send()
    own = pltpu.roll(value, lax.rem(128 - lax.rem(fs, 4) * SHARD, 128), 1)
    flipped = jnp.concatenate([own, jnp.zeros((112, 128), F32)], axis=0).T
    first_grad[...] = flipped[0:SHARD, 0:TAPS]
    for ref, at in zip((vec_b, vec_g, vec_s, vec_b2, vec_g2, vec_s2), range(10, 16)):
        ref[...] = own[at : at + 1, 0:SHARD]


def whole(shape):
    return pl.BlockSpec(shape, lambda i: (0,) * len(shape))


def local(
    waveforms, packing_list, segment_ids, first_weight, first_bias, first_gain, first_shift,
    second_weight, second_bias, second_gain, second_shift, cotangent,
):
    vecs = jnp.stack([first_bias, first_gain, first_shift, second_bias, second_gain, second_shift])
    mask, pick = patch_tables()
    shape = jax.ShapeDtypeStruct
    dma = pltpu.SemaphoreType.DMA
    rows = lambda width: pl.BlockSpec((TILE, width), lambda i: (i, 0))
    wide = shape((ROWS, CH), BF16)
    narrow = shape((ROWS, 128), BF16)
    anywhere = pl.BlockSpec(memory_space=pl.ANY)
    he, ho, de, do, le, lo, small, second = pl.pallas_call(
        first_kernel,
        grid=(STEPS,),
        out_shape=[wide, wide, wide, wide, narrow, narrow, shape((16, CH), F32), shape((CH, 3 * CH), BF16)],
        in_specs=[
            whole((4, 128)), whole((1, 128)), whole((1, FRAMES, 320)), whole((SHARD, TAPS)), whole((6, SHARD)),
            whole((SHARD, 3 * CH)), whole((TILE + 16, 384)), whole((384, 384)),
        ],
        out_specs=[rows(CH), rows(CH), rows(CH), rows(CH), rows(128), rows(128), whole((16, CH)), anywhere],
        scratch_shapes=[
            pltpu.VMEM((128, 320), BF16), pltpu.VMEM((128, 320), BF16),
            pltpu.VMEM((16, 128), BF16), pltpu.VMEM((FS, 16, 128), BF16),
            pltpu.VMEM((CH, 3 * CH), BF16), pltpu.VMEM((144, 384), F32),
            pltpu.VMEM((128, CH), BF16), pltpu.VMEM((128, 256), F32),
            dma((DP,)), dma((DP,)), dma((FS,)), dma((FS,)), dma((FS,)), dma((FS,)), dma((FS,)), dma((FS,)), dma,
        ],
        compiler_params=pltpu.CompilerParams(
            collective_id=0, has_side_effects=True, vmem_limit_bytes=48 << 20
        ),
    )(packing_list, segment_ids, waveforms, first_weight, vecs, second_weight, mask, pick)

    features, g1, gs, sums = pl.pallas_call(
        second_kernel,
        grid=(STEPS,),
        out_shape=[shape((1, ROWS, CH), BF16), wide, wide, shape((24, CH), F32)],
        in_specs=[
            rows(CH), rows(CH),
            pl.BlockSpec((16, CH), lambda i: (jnp.minimum((i + 1) * (TILE // 16), ROWS // 16 - 1), 0)),
            rows(128), pl.BlockSpec((1, TILE, CH), lambda i: (0, i, 0)),
            whole((CH, 3 * CH)), whole((16, CH)),
        ],
        out_specs=[pl.BlockSpec((1, TILE, CH), lambda i: (0, i, 0)), rows(CH), rows(CH), whole((24, CH))],
        scratch_shapes=[pltpu.VMEM((8, CH), F32)],
        compiler_params=pltpu.CompilerParams(vmem_limit_bytes=48 << 20),
    )(he, ho, he, lo, cotangent, second, small)

    vmem = pl.BlockSpec(memory_space=pltpu.VMEM)
    one = shape((1, SHARD), F32)
    second_grad, first_grad, b1, n1, s1, b2, n2, s2 = pl.pallas_call(
        third_kernel,
        out_shape=[shape((SHARD, 3 * CH), F32), shape((SHARD, TAPS), F32)] + [one] * 6,
        in_specs=[anywhere] * 8 + [vmem] * 3,
        out_specs=[vmem] * 8,
        scratch_shapes=[pltpu.VMEM((ROWS, CH), BF16)] * 6
        + [pltpu.VMEM((ROWS, 128), BF16)] * 2
        + [
            pltpu.VMEM((CH, 3 * CH), F32), pltpu.VMEM((FS, 2, 16, 3 * CH), BF16),
            pltpu.VMEM((FS, 16, 3 * CH), BF16), pltpu.VMEM((FS, 16, 3 * CH), BF16),
            pltpu.VMEM((4, FS, 16, 384), BF16), pltpu.VMEM((FS, 16, 384), F32),
            pltpu.VMEM((FS, 16, 384), F32), pltpu.VMEM((16, 384), F32),
            pltpu.VMEM((SHARD, 3 * CH), F32), pltpu.VMEM((128, CH), BF16),
            pltpu.VMEM((128, CH), F32), pltpu.VMEM((128, 128), F32),
            pltpu.VMEM((4, 16, 128), F32), pltpu.VMEM((FS, 16, 128), F32),
            pltpu.VMEM((16, 128), F32), pltpu.VMEM((DP, 16, 128), F32),
            dma((8, 4)), dma((4,)), dma((4,)), dma((4,)), dma((4,)), dma((FS,)), dma((FS,)),
            dma((DP,)), dma((DP,)), dma((FS,)), dma((FS,)), dma((DP,)), dma((DP,)),
        ],
        compiler_params=pltpu.CompilerParams(
            collective_id=1, has_side_effects=True, vmem_limit_bytes=56 << 20
        ),
    )(he, ho, g1, gs, de, do, le, lo, second, small, sums)
    flat = lambda value: value.reshape(SHARD)
    return (
        features, first_grad, flat(b1), flat(n1), flat(s1), second_grad, flat(b2), flat(n2), flat(s2),
    )


def solution(mesh):
    placed = (
        P("dp", "fsdp", None), P(None, "fsdp"), P("dp", "fsdp"), P("fsdp", None), P("fsdp"), P("fsdp"),
        P("fsdp"), P("fsdp", None), P("fsdp"), P("fsdp"), P("fsdp"), P("dp", "fsdp", None),
    )
    out = (
        P("dp", "fsdp", None), P("fsdp", None), P("fsdp"), P("fsdp"), P("fsdp"), P("fsdp", None),
        P("fsdp"), P("fsdp"), P("fsdp"),
    )
    return jax.shard_map(local, mesh=mesh, in_specs=placed, out_specs=out, check_vma=False)
```

time: 539 us -> 135 us (0.25); the launches traced: 530 us -> 134 us
  other arithmetic: 166 us -> 0 us
  blocking collectives: 165 us -> 0 us
  Pallas kernels: 0 us -> 115 us
  local copies, waits for them, and re-layouts: 105 us -> 18.2 us
  matrix products: 52.8 us -> 0 us
  waiting for transfers between devices: 25.2 us -> 0 us
  between operations: 15.8 us -> 0.7 us
    pallas_call x0 -> x3, Pallas kernels: none -> 115 us  [the longest x1 56.4 us: local(): pl.pallas_call(third_kernel, out_shape=[shape((SHARD, 3 * CH), F32), shap...]
    reduce_sum x10 -> x0, other arithmetic: 102 us -> none  [the longest x2 57.2 us: norm_act(): scaled = centred * lax.rsqrt(spread + epsilon) * scale_by + shift_by]
    unnamed x2 -> x0, blocking collectives: 93.4 us -> none
    reshape x3 -> x0, local copies, waits for them, and re-layouts: 49.1 us -> none  [the longest x2 35.8 us: local_pass(): grad_hidden = (grad_columns[:, :2 * channels] + jnp.concatenate([shifted,...]
    dot_general x4 -> x0, matrix products: 44.1 us -> none  [the longest x1 14.6 us: local_pass(): jnp.dot(grad_second, kernel_two, preferred_element_type=jnp.float32)]
    convert_element_type x9 -> x0, other arithmetic: 43.3 us -> none  [the longest x1 43.1 us: local_pass(): hidden = post_first.astype(jnp.bfloat16)]
    psum x1 -> x0, blocking collectives: 41 us -> none  [local(): lax.psum((second_part, summed[0], summed[1], summed[2], summed[3], summed...]
    all_gather x2 -> x0, blocking collectives: 30.7 us -> none  [the longest x1 15.4 us: local(): lax.all_gather(first_weight, 'fsdp', axis=0, tiled=True)]
  transfers between devices with their start and end apart: 4 -> 0, of which waited for: 2 -> 0; matrix products, arithmetic and copies ran while one was open for 49% -> 0% of each run, Pallas kernels for 0% -> 0%
where the time goes in v1:
time: 135 us; the launch traced here: 134 us
  Pallas kernels  115 us (85%)
  local copies, waits for them, and re-layouts  18.2 us (13%)
    pallas_call x1, Pallas kernels, local(): pl.pallas_call(third_kernel, out_shape=[shape((SHARD, 3 * CH), F32), shap...  56.4 us
    pallas_call x1, Pallas kernels, local(): pl.pallas_call(first_kernel, grid=(STEPS,), out_shape=[wide, wide, wide,...  35.2 us
    pallas_call x1, Pallas kernels, local(): pl.pallas_call(second_kernel, grid=(STEPS,), out_shape=[shape((1, ROWS, C...  23.4 us
    unnamed x30, local copies, waits for them, and re-layouts  17.4 us

profile of v1, /device:TPU:1, one launch (start us, length us, event | category | flops | bytes accessed | tf_op | source)
XLA Modules:
  0.0 134.0 jit_solution(12113630997187723824)
XLA Ops:
  0.6 1.0 copy.23.wave_ref
  1.6 0.8 copy.24.weight_ref
  2.4 0.8 stack.27.vec_ref
  3.2 0.0 copy-start.3
  3.2 1.0 copy-done.3
  4.2 0.0 copy-start.4
  4.2 0.9 copy-done.4
  5.1 0.0 copy-start.6
  5.1 0.9 copy-done.6
  6.0 0.0 copy-start.8
  6.0 0.7 copy-done.8
  6.7 0.0 copy-start.9
  6.7 0.7 copy-done.9
  7.3 35.2 %shard_map.205 = (bf16[4096,512]{1,0:T(8,128)(2,1)}, bf16[4096,512]{1,0:T(8,128)(2,1)}, bf16[4096,512]{1,0:T(8,128)(2,1)}, bf16[4096,512]{1,0:T(8,128)(2,1)}, bf...) custom-call(s32[4,128]{1,0:T(4,128)S(1)} %copy-done.8, ...), custom_call_target="tpu_custom_call" | custom-call | tf_op jit(solution)/shard_map/pallas_call | solution.py:530
  42.6 0.0 copy-start.2
  42.6 1.0 copy-done.2
  43.5 0.0 copy-start
  43.6 23.4 %shard_map.206 = (bf16[1,4096,512]{2,1,0:T(8,128)(2,1)}, bf16[4096,512]{1,0:T(8,128)(2,1)}, bf16[4096,512]{1,0:T(8,128)(2,1)}, f32[24,512]{1,0:T(8,128)S(1)}) custom-call(bf16[4096,512]{1,0:T(8,128)(2,1)} %get-tuple-element.29.he_ref.halo_ref.he_in, bf16[4096,512]{1,0:T(8,128)(2,1)} %get-tuple-element.30.ho_ref.ho_in, ...), custom_call_target="tpu_custom_call" | custom-call | tf_op jit(solution)/shard_map/pallas_call | solution.py:551
  67.0 0.0 copy-done
  67.0 0.0 copy-done.1
  67.0 0.0 copy-done.5
  67.0 0.0 copy-start.7
  67.0 0.6 copy-done.7
  67.6 56.4 %shard_map.207 = (f32[32,1536]{1,0:T(8,128)}, f32[32,10]{1,0:T(8,128)}, f32[1,32]{1,0:T(1,128)}, f32[1,32]{1,0:T(1,128)}, f32[1,32]{1,0:T(1,128)}, /*index=5*/f3...) custom-call(bf16[4096,512]{1,0:T(8,128)(2,1)} %get-tuple-element.29.he_ref.halo_ref.he_in, ...), custom_call_target="tpu_custom_call" | custom-call | tf_op jit(solution)/shard_map/pallas_call | solution.py:568
  124.0 1.4 %copy.25 = f32[32,10]{0,1:T(8,128)} copy(f32[32,10]{1,0:T(8,128)} %get-tuple-element.50) | data formatting | bytes 2560
  125.4 1.1 copy.33
  126.6 1.1 copy.34
  127.7 1.2 copy.35
  128.8 1.6 %copy.36 = f32[32,1536]{1,0:T(8,128)} copy(f32[32,1536]{1,0:T(8,128)} %get-tuple-element.72) | data formatting | bytes 393216
  130.4 1.2 copy.37
  131.6 1.2 copy.38
  132.8 1.1 copy.39
  (2 shorter events, 0.0 us)
Async XLA Ops:
  3.2 1.0 copy-start.3
  4.2 0.9 copy-start.4
  5.1 0.9 copy-start.6
  6.0 0.7 copy-start.8
  6.7 0.7 copy-start.9
  42.6 1.0 copy-start.2
  43.5 23.4 %copy-start = (bf16[512,1536]{1,0:T(8,128)(2,1)}, bf16[512,1536]{1,0:T(8,128)(2,1)S(1)}, u32[]{:S(2)}) copy-start(bf16[512,1536]{1,0:T(8,128)(2,1)S(1)} %get-tuple-element.32.weight_ref) | copy-start | bytes 4718596
  43.6 23.4 %copy-start.1 = (bf16[4096,128]{1,0:T(8,128)(2,1)}, bf16[4096,128]{1,0:T(8,128)(2,1)S(1)}, u32[]{:S(2)}) copy-start(bf16[4096,128]{1,0:T(8,128)(2,1)S(1)} %get-tuple-element.31.lo_ref.lo_in) | copy-start | bytes 3145732
  43.6 23.4 %copy-start.5 = (f32[16,512]{1,0:T(8,128)}, f32[16,512]{1,0:T(8,128)S(1)}, u32[]{:S(2)}) copy-start(f32[16,512]{1,0:T(8,128)S(1)} %get-tuple-element.33.small_ref) | copy-start | bytes 98308
  67.0 0.6 copy-start.7

commit v2 on v0

v2 whole, which is shorter than its diff:
```python
import jax
import jax.numpy as jnp
from jax import lax
from jax.experimental import pallas as pl
from jax.experimental.pallas import tpu as pltpu
from jax.sharding import PartitionSpec as P

MESH = pl.DeviceIdType.MESH
F32, BF16, I32 = jnp.float32, jnp.bfloat16, jnp.int32
EXACT = lax.Precision.HIGHEST
CH, FRAMES, ROWS, TILE, STEPS = 512, 128, 4096, 512, 8
PER_STEP = TILE // 32
PART = 256
VMEM_LIMIT = 60 << 20
FIRST, SECOND = STEPS, 2 * STEPS + 2
DP, FS = 8, 16
SHARD, SLOT, TAPS = 32, 16, 10
EPS = 1e-05
HALF = 0.7071067811865476
EXP_BY = -1.4426950408889634
EXP_PLUS = -0.32574806470870245


def mm(a, b, dims, precision=None):
    return lax.dot_general(
        a, b, (dims, ((), ())), precision=precision, preferred_element_type=F32
    )


def iota(shape, axis):
    return lax.broadcasted_iota(I32, shape, axis)


def patch_mask():
    shape = (TILE + 16, 384)
    lane = iota(shape, 1)
    at = iota(shape, 0) % 32
    first = at * TAPS
    on = (lane >= first) & (lane < first + TAPS) & (lane < 320)
    on |= lane == 320
    on |= (lane == 321) & (at != 31)
    on |= (lane == 322) & (at == 31)
    return jnp.where(on, 1.0, 0.0).astype(BF16)


def patch_pick():
    shape = (384, 384)
    sample = iota(shape, 0)
    out = iota(shape, 1)
    tap = sample - TAPS * ((sample * 6554) // 65536)
    block = out // 128
    lane = out % 128
    group = lane % 16
    within = (lane < 48) & (sample < 320)
    on = (block == 0) & (group < TAPS) & (tap == group)
    on |= (block == 1) & (group < 5) & (tap == group + 5)
    on |= (block == 2) & (group >= 5) & (group < TAPS) & (tap == group - 5)
    on &= within
    flag = (lane == 48) | (lane == 49)
    on |= flag & (block == 0) & (sample == 320)
    on |= flag & (block == 1) & ((sample == 321) | (sample == 322))
    return jnp.where(on, 1.0, 0.0).astype(BF16)


def along_x(fs, k):
    return fs // 4 * 4 + lax.rem(fs + k, 4)


def along_z(fs, k):
    return lax.rem(fs + 4 * k, FS)


def greet(dp, fs):
    barrier = pltpu.get_barrier_semaphore()
    for k in range(1, DP):
        pl.semaphore_signal(barrier, inc=1, device_id=(lax.rem(dp + k, DP), fs), device_id_type=MESH)
    for k in range(1, 4):
        pl.semaphore_signal(barrier, inc=1, device_id=(dp, along_x(fs, k)), device_id_type=MESH)
        pl.semaphore_signal(barrier, inc=1, device_id=(dp, along_z(fs, k)), device_id_type=MESH)


def all_here():
    pl.semaphore_wait(pltpu.get_barrier_semaphore(), DP - 1 + 6)


def send(src, dst, send_sem, recv_sem, device):
    return pltpu.make_async_remote_copy(
        src_ref=src, dst_ref=dst, send_sem=send_sem, recv_sem=recv_sem,
        device_id=device, device_id_type=MESH,
    )


def centred_weights(small):
    centred = small - jnp.mean(small, axis=1, keepdims=True)
    return jnp.where(iota((16, CH), 0) <= TAPS, centred, 0.0)


def split(value):
    high = value.astype(BF16).astype(F32)
    return high, value - high


def tile_rows(index):
    return pl.ds(pl.multiple_of(index * TILE, TILE), TILE)


def main_kernel(
    list_ref, seg_ref, wave_ref, weight_ref, vec_0, vec_1, vec_2, vec_3, vec_4, vec_5, second_ref, cot_ref,
    feat_ref, second_grad, vec_grad,
    slots, heard, part_own, smalls, part_row, part_rows, second_all, frames, rhs, quad, mask_ref, pick_ref, patches,
    small_ref, he, ho, de, do, le, lo, g1, gs,
    carry, total, sums_ref, pre_0, pre_1, g_0, g_1, gs_0, gs_1, grad_ref,
    even_0, even_1, odd_0, odd_1, pair_in, pair_sum, near_a, near_b, sum_a, sum_b,
    far_a, far_b, f_all, y_in, f_sum, gathered, wz, t_acc, r_acc,
    small_own, small_z, small_zsum, small_x, small_sum, small_dp,
    a2a_s, a2a_r, sm_s, sm_r, sz_0, sz_1, w_s, w_r, v_s, v_r, fw_s, fw_r,
    p_s, p_r, n_s, n_r, m_s, m_r, y_s, y_r, d_s, d_r, sz_s, sz_r, sx_s, sx_r, e_s, e_r,
):
    step = pl.program_id(0)
    dp, fs = lax.axis_index("dp"), lax.axis_index("fsdp")
    core = lax.rem(dp, 2)
    yy = dp // 2
    zz, xx = fs // 4, lax.rem(fs, 4)
    sibling = dp + 1 - 2 * core
    half = pl.ds(pl.multiple_of(core * 768, 128), 768)
    quarter = pl.ds(pl.multiple_of(yy * 384, 128), 384)
    pres, gs_pair = (pre_0, pre_1), ((g_0, gs_0), (g_1, gs_1))
    spreads = ((even_0, odd_0), (even_1, odd_1))

    def a2a_copy(k):
        target = lax.rem(dp + k, DP)
        return send(
            slots.at[pl.ds(pl.multiple_of(target * SLOT, SLOT), SLOT)],
            heard.at[pl.ds(pl.multiple_of(dp * SLOT, SLOT), SLOT)],
            a2a_s.at[k], a2a_r.at[k], (target, fs),
        )

    w_cols_a = pl.ds(pl.multiple_of(core * 768, 128), 384)
    w_cols_b = pl.ds(pl.multiple_of(core * 768 + 384, 128), 384)

    def part_x(k):
        return send(part_own, smalls.at[k], sm_s.at[k], sm_r.at[k], (dp, along_x(fs, k)))

    def part_z(k):
        return send(part_row, part_rows.at[zz], sz_0.at[k], sz_1.at[k], (dp, along_z(fs, k)))

    def near_weights(k):
        return (
            send(second_ref.at[:, w_cols_a], second_all.at[zz, xx, :, w_cols_a], w_s.at[0, k], w_r.at[0, k], (dp, along_x(fs, k))),
            send(second_ref.at[:, w_cols_b], second_all.at[zz, xx, :, w_cols_b], w_s.at[1, k], w_r.at[1, k], (dp, along_z(fs, k))),
        )

    def far_weights(k):
        piece_a = second_all.at[zz, :, :, w_cols_a]
        piece_b = second_all.at[:, xx, :, w_cols_b]
        return (
            send(piece_a, piece_a, v_s.at[0, k], v_r.at[0, k], (dp, along_z(fs, k))),
            send(piece_b, piece_b, v_s.at[1, k], v_r.at[1, k], (dp, along_x(fs, k))),
        )

    def forward_copy():
        piece = second_all.at[:, :, :, half]
        return send(piece, piece, fw_s, fw_r, (sibling, fs))

    @pl.when(step == 0)
    def _():
        greet(dp, fs)
        sums_ref[...] = jnp.zeros_like(sums_ref)
        carry[...] = jnp.zeros_like(carry)
        total[...] = jnp.zeros_like(total)
        he[ROWS:] = jnp.zeros((16, CH), BF16)
        t_acc[...] = jnp.zeros_like(t_acc)
        r_acc[...] = jnp.zeros_like(r_acc)
        table = list_ref[...].astype(F32)
        eye = iota((128, 128), 0) == iota((128, 128), 1)

        def row(i):
            return jnp.broadcast_to(table[i : i + 1], (128, 128))

        def col(value):
            return jnp.sum(jnp.where(eye, value, 0.0), axis=1, keepdims=True)

        source, owner, place, length = row(0), row(1), row(2), row(3)
        source_c, owner_c, length_c = col(source), col(owner), col(length)
        earlier = (iota((128, 128), 0) < iota((128, 128), 1)) & (source_c == source)
        read_at = jnp.sum(jnp.where(earlier, length_c, 0.0), axis=0, keepdims=True)
        slot_at = jnp.sum(
            jnp.where(earlier & (owner_c == owner), length_c, 0.0), axis=0, keepdims=True
        )
        read_at = jnp.broadcast_to(read_at, (128, 128))
        slot_at = jnp.broadcast_to(slot_at, (128, 128))
        row_at = iota((128, 128), 0)
        lane_f = iota((128, 128), 1).astype(F32)
        group = (row_at // SLOT).astype(F32)
        inner = (row_at % SLOT).astype(F32)
        me = dp.astype(F32)
        entry = (
            (owner == group) & (source == me)
            & (slot_at <= inner) & (inner < slot_at + length)
        )
        frame = jnp.sum(jnp.where(entry, read_at + inner - slot_at + 1.0, 0.0), axis=1, keepdims=True)
        pack = jnp.where(lane_f + 1.0 == frame, 1.0, 0.0).astype(BF16)
        slots[...] = mm(pack, wave_ref[...], ((1,), (1,))).astype(BF16)

        place_lanes = jnp.where(
            iota((SHARD, 128), 1) == iota((SHARD, 128), 0) + lax.rem(fs, 4) * SHARD, 1.0, 0.0
        ).astype(BF16)
        quad[0:TAPS, 0:128] = mm(weight_ref[...], place_lanes, ((1,), (0,)))
        frames[0:8, 0:128] = jnp.zeros((8, 128), F32)
        for at, ref in enumerate((vec_0, vec_1, vec_2, vec_3, vec_4, vec_5)):
            frames[at : at + 1, 0:SHARD] = ref[...].astype(F32)
        vecs = frames[0:8, 0:SHARD].astype(BF16)
        quad[TAPS:16, 0:128] = mm(vecs, place_lanes, ((1,), (0,)))[0:6]
        part_own[...] = quad[0:16, 0:128].astype(BF16)

        all_here()
        for k in range(1, 4):
            part_x(k).start()
        for k in range(1, DP):
            a2a_copy(k).start()
        for k in range(1, 4):
            for copy in near_weights(k):
                copy.start()
        mask_ref[...] = patch_mask()
        whole_row = part_own[...].astype(F32)
        for k in range(1, 4):
            part_x(k).wait_recv()
            whole_row = whole_row + smalls[k].astype(F32)
        part_row[...] = whole_row.astype(BF16)
        for k in range(1, 4):
            part_z(k).start()
        pick_ref[...] = patch_pick()
        mine = pl.ds(pl.multiple_of(dp * SLOT, SLOT), SLOT)
        heard[mine] = slots[mine]
        second_all[zz, xx, :, half] = second_ref[:, half]

        position = row_at.astype(F32)
        entry = (owner == me) & (position >= place) & (position < place + length)
        origin = jnp.sum(
            jnp.where(entry, source * SLOT + slot_at + position - place + 1.0, 0.0),
            axis=1, keepdims=True,
        )
        unpack = jnp.where(lane_f + 1.0 == origin, 1.0, 0.0).astype(BF16)
        seg = jnp.broadcast_to(seg_ref[...].astype(F32), (128, 128))
        following = jnp.where(iota((128, 128), 1) == 127, -1.0, pltpu.roll(seg, 127, 1))
        inside = jnp.where(seg >= 0, 1.0, 0.0)
        inside_c = col(inside)
        kept_c = col(jnp.where(following != seg, 0.0, inside))
        lane = iota((128, 128), 1)
        flags = jnp.where(
            (lane == 64) | (lane == 65), inside_c, jnp.where(lane == 66, kept_c, 0.0)
        )

        for k in range(1, DP):
            a2a_copy(k).wait_recv()
        packed = mm(unpack, heard[...], ((1,), (0,)))
        frames[0:128, 256:384] = flags
        frames[0:128, 0:320] = packed
        frames[128:144, :] = jnp.zeros((16, 384), F32)
        def cut(turn, _):
            few = frames[pl.ds(pl.multiple_of(turn * PER_STEP, PER_STEP), 32)].astype(BF16)
            spread = iota((TILE + 16, 32), 0)
            start = iota((TILE + 16, 32), 1) * 32
            repeat = jnp.where((spread >= start) & (spread < start + 32), 1.0, 0.0).astype(BF16)
            wide = mm(repeat, few, ((1,), (0,))).astype(BF16) * mask_ref[...]
            taken = mm(wide, pick_ref[...], ((1,), (0,)))
            even = taken[:TILE, 0:128]
            odd = taken[:TILE, 128:256] + pltpu.roll(taken[:, 256:384], TILE + 15, 0)[:TILE]
            lane1 = iota((1, 128), 1)
            bias_lane = jnp.where((lane1 == 10) | (lane1 == 26) | (lane1 == 42), 1.0, 0.0)
            patches[turn] = (jnp.concatenate([even, odd], axis=0) + bias_lane).astype(BF16)
            return 0

        lax.fori_loop(0, STEPS, cut, 0)

        part_rows[pl.ds(zz, 1)] = part_row[...][None]
        for k in range(1, 4):
            part_z(k).wait_recv()
        small = jnp.concatenate([part_rows[g].astype(F32) for g in range(4)], axis=1)
        small_ref[...] = small
        centred = centred_weights(small)
        high, low = split(centred * small[11:12] * HALF)
        shift_high, shift_low = split(small[12:13] * HALF)
        r16 = iota((16, CH), 0)
        shifts = jnp.where(r16 == 0, shift_high, jnp.where(r16 == 1, shift_low, 0.0))
        rhs[...] = jnp.concatenate(
            [high, low, high, shifts, jnp.zeros((64, CH), F32)], axis=0
        ).astype(BF16)
        wide = jnp.concatenate([centred, jnp.zeros((112, CH), F32)], axis=0)
        gram = mm(centred, wide, ((1,), (1,)), EXACT) * (1.0 / CH)
        gram_a, rest = split(gram)
        gram_b, gram_c = split(rest)
        quad[:, 0:128] = jnp.concatenate(
            [gram_a, gram_b, gram_c, jnp.zeros((80, 128), F32)], axis=0
        )
        quad[:, 128:256] = jnp.where(row_at == 48, 1.0, 0.0)

    @pl.when(step < STEPS)
    def _():
        patch_bf = patches[step]
        patch = patch_bf.astype(F32)
        form = mm(patch_bf, quad[...].astype(BF16), ((1,), (0,)))
        var = jnp.sum(form[:, 0:128] * patch, axis=1, keepdims=True)
        scale = lax.rsqrt(jnp.maximum(var, 0.0) + EPS) * form[:, 128:256]
        scaled = patch * scale
        high, low = split(scaled)
        lane_t = iota((2 * TILE, 128), 1)
        left = jnp.where(lane_t < 32, high, jnp.where(lane_t < 48, low, patch)).astype(BF16)
        rows = tile_rows(step)
        for part, (h_ref, d_ref, l_ref) in enumerate(((he, de, le), (ho, do, lo))):
            piece = left[part * TILE : (part + 1) * TILE]
            l_ref[rows] = piece
            u = mm(piece, rhs[...], ((1,), (0,)))
            phi = HALF * lax.erf(u) + HALF
            h_ref[rows] = (u * phi).astype(BF16)
            bell = jnp.exp2(u * u * EXP_BY + EXP_PLUS)
            d_ref[rows] = (phi + u * bell).astype(BF16)

    @pl.when(step == 1)
    def _():
        for k in range(1, 4):
            for copy in near_weights(k):
                copy.wait_recv()
        for k in range(1, 4):
            for copy in far_weights(k):
                copy.start()

    @pl.when(step == STEPS - 3)
    def _():
        for k in range(1, 4):
            for copy in far_weights(k):
                copy.wait_recv()
        forward_copy().start()

    @pl.when(step == STEPS - 1)
    def _():
        forward_copy().wait_recv()
        for k in range(1, DP):
            a2a_copy(k).wait_send()
        for k in range(1, 4):
            part_x(k).wait_send()
            part_z(k).wait_send()
            for copy in near_weights(k) + far_weights(k):
                copy.wait_send()
        forward_copy().wait_send()

    def pair_copy(m):
        return send(grad_ref.at[m, :, 1 - core], pair_in.at[m], p_s.at[m], p_r.at[m], (sibling, fs))

    cols_a, cols_b = pl.ds(0, 768), pl.ds(768, 768)

    def near_copies(k):
        z_to, x_to = lax.rem(zz + k, 4), lax.rem(xx + k, 4)
        return (
            send(pair_sum.at[z_to, :, :, cols_a], near_a.at[k], n_s.at[0, k], n_r.at[0, k], (dp, along_z(fs, k))),
            send(pair_sum.at[:, x_to, :, cols_b], near_b.at[k], n_s.at[1, k], n_r.at[1, k], (dp, along_x(fs, k))),
        )

    def far_copies(k):
        z_to, x_to = lax.rem(zz + k, 4), lax.rem(xx + k, 4)
        return (
            send(sum_a.at[x_to], far_a.at[k], m_s.at[0, k], m_r.at[0, k], (dp, along_x(fs, k))),
            send(sum_b.at[z_to], far_b.at[k], m_s.at[1, k], m_r.at[1, k], (dp, along_z(fs, k))),
        )

    def y_copy(k):
        target = lax.rem(yy + k, 4)
        return send(
            f_all.at[:, pl.ds(pl.multiple_of(target * 384, 128), 384)], y_in.at[k],
            y_s.at[k], y_r.at[k], (target * 2 + core, fs),
        )

    def d_copy(k):
        rows = pl.ds(pl.multiple_of(core * 16, 16), 16)
        return send(f_sum, gathered.at[rows, quarter], d_s.at[k], d_r.at[k], (lax.rem(dp + k, DP), fs))

    def sz_copy(k):
        return send(small_own.at[lax.rem(zz + k, 4)], small_z.at[k], sz_s.at[k], sz_r.at[k], (dp, along_z(fs, k)))

    def sx_copy(k):
        return send(small_zsum, small_x.at[k], sx_s.at[k], sx_r.at[k], (dp, along_x(fs, k)))

    def e_copy(k):
        return send(small_sum, small_dp.at[k], e_s.at[k], e_r.at[k], (lax.rem(dp + k, DP), fs))

    def taps(c):
        return second_all[:, :, :, c * CH : (c + 1) * CH].reshape(CH, CH)

    def convolve(slot):
        rows = tile_rows(step - FIRST)
        more = pl.ds(pl.multiple_of((step - FIRST) * TILE, TILE), TILE + 16)
        pre = mm(he[rows], taps(0), ((1,), (1,))) + mm(ho[rows], taps(1), ((1,), (1,)))
        third = mm(he[more], taps(2), ((1,), (1,)))
        pres[slot][...] = pre + pltpu.roll(third, TILE + 15, 0)[:TILE]

    def activate(slot):
        bias, gain, shift = small_ref[13:14], small_ref[14:15], small_ref[15:16]
        gain_u, shift_u = gain * HALF, shift * HALF
        last = carry[0:1]
        totals = [jnp.zeros((8, CH), F32)] * 3
        for part in range(TILE // PART):
            rows = pl.ds(part * PART, PART)
            far = pl.ds(pl.multiple_of((step - FIRST - 1) * TILE + part * PART, PART), PART)
            keep = lo[far].astype(F32)[:, 48:49]
            pre = pres[slot][rows] + bias
            centred = pre - jnp.mean(pre, axis=1, keepdims=True)
            var = jnp.mean(centred * centred, axis=1, keepdims=True)
            scale = lax.rsqrt(var + EPS)
            norm = centred * scale
            u = norm * gain_u + shift_u
            phi = HALF * lax.erf(u) + HALF
            feat_ref[0, rows] = (u * phi * keep).astype(BF16)
            bell = jnp.exp2(u * u * EXP_BY + EXP_PLUS)
            slope = phi + u * bell
            dnorm = cot_ref[0, rows].astype(F32) * (keep * HALF) * slope * gain
            prod = dnorm * norm
            mean_a = jnp.mean(dnorm, axis=1, keepdims=True)
            mean_b = jnp.mean(prod, axis=1, keepdims=True)
            dpre = (dnorm - mean_a - norm * mean_b) * scale
            for at, value in enumerate((dpre, prod, dnorm)):
                totals[at] = totals[at] + jnp.sum(value.reshape(PART // 8, 8, CH), axis=0)
            g1[far] = dpre.astype(BF16)
            gs_pair[slot][0][rows] = dpre.astype(BF16)
            rolled = pltpu.roll(dpre, 1, 0)
            rolled = jnp.where(iota((PART, CH), 0) == 0, last, rolled).astype(BF16)
            gs[far] = rolled
            gs_pair[slot][1][rows] = rolled
            last = dpre[PART - 1 : PART]
        carry[0:1] = last
        for at in range(3):
            sums_ref[at * 8 : at * 8 + 8] += totals[at]

    def weigh(slot):
        g_part, gs_part = gs_pair[slot]
        rows = tile_rows(step - FIRST - 2)
        for c, (left, right) in enumerate(((g_part, he), (g_part, ho), (gs_part, he))):
            total[:, c * CH : (c + 1) * CH] += mm(left[...], right[rows], ((0,), (0,)))

    at = step - FIRST

    @pl.when(at == 0)
    def _():
        convolve(0)

    @pl.when(at == 1)
    def _():
        convolve(1)
        activate(0)

    for slot in range(2):

        @pl.when((at >= 2) & (at < STEPS) & (at % 2 == slot))
        def _(slot=slot):
            convolve(slot)
            weigh(slot)
            activate(1 - slot)

    @pl.when(at == STEPS)
    def _():
        weigh(0)
        activate(1)

    @pl.when(at == STEPS + 1)
    def _():
        weigh(1)
        grad_ref[...] = total[...].astype(BF16).reshape(4, 4, 2, 16, 3 * CH)
        for m in range(4):
            pair_copy(m).start()

    def spread(slot):
        rows = tile_rows(step - SECOND)
        g_tile = g1[rows]
        even = mm(g_tile, taps(0), ((1,), (0,)))
        spreads[slot][0][...] = even + mm(gs[rows], taps(2), ((1,), (0,)))
        spreads[slot][1][...] = mm(g_tile, taps(1), ((1,), (0,)))

    def gather_terms(slot):
        lane = iota((TILE, 128), 1)
        rows = tile_rows(step - SECOND - 1)
        for d_hidden, slope, lhs in zip(spreads[slot], (de, do), (le, lo)):
            ds = (d_hidden[...] * slope[rows].astype(F32)).astype(BF16)
            left = lhs[rows]
            left_f = left.astype(F32)
            z = mm(ds, wz[...], ((1,), (1,)))
            inner = jnp.where(lane < 48, z * left_f, 0.0)
            corr = jnp.sum(inner, axis=1, keepdims=True)
            y = jnp.where(lane < 48, corr * left_f, z).astype(BF16)
            t_acc[...] += mm(left, ds, ((0,), (0,)))
            r_acc[...] += mm(y, left, ((0,), (0,)))

    then = step - SECOND

    @pl.when(then == 0)
    def _():
        small = small_ref[...]
        gain = small[11:12]
        high, low = split(centred_weights(small) * gain)
        wz[...] = jnp.concatenate(
            [high, low, high, jnp.where(iota((16, CH), 0) == 0, gain, 0.0), jnp.zeros((64, CH), F32)], axis=0
        ).astype(BF16)
        spread(0)

    for slot in range(2):

        @pl.when((then >= 1) & (then < STEPS) & (then % 2 == slot))
        def _(slot=slot):
            spread(slot)
            gather_terms(1 - slot)

    @pl.when(then == 1)
    def _():
        for m in range(4):
            pair_copy(m).wait_recv()
            pair_sum[m] = (grad_ref[m, :, core].astype(F32) + pair_in[m].astype(F32)).astype(BF16)
        for k in range(1, 4):
            for copy in near_copies(k):
                copy.start()

    @pl.when(then == 5)
    def _():
        value_a = pair_sum[zz, :, :, cols_a].astype(F32)
        value_b = pair_sum[:, xx, :, cols_b].astype(F32)
        for k in range(1, 4):
            for copy in near_copies(k):
                copy.wait_recv()
            value_a = value_a + near_a[k].astype(F32)
            value_b = value_b + near_b[k].astype(F32)
        sum_a[...] = value_a.astype(BF16)
        sum_b[...] = value_b.astype(BF16)
        for k in range(1, 4):
            for copy in far_copies(k):
                copy.start()

    @pl.when(then == 6)
    def _():
        value_a = sum_a[xx].astype(F32)
        value_b = sum_b[zz].astype(F32)
        for k in range(1, 4):
            for copy in far_copies(k):
                copy.wait_recv()
            value_a = value_a + far_a[k].astype(F32)
            value_b = value_b + far_b[k].astype(F32)
        f_all[:, cols_a] = value_a
        f_all[:, cols_b] = value_b
        for k in range(1, 4):
            y_copy(k).start()

    @pl.when(then == 7)
    def _():
        value = f_all[:, quarter]
        for k in range(1, 4):
            y_copy(k).wait_recv()
            value = value + y_in[k]
        f_sum[...] = value
        for k in range(1, DP):
            d_copy(k).start()

    @pl.when(then == STEPS)
    def _():
        gather_terms(1)
        small = small_ref[...]
        centred = centred_weights(small)
        gain = small[11:12]
        r16 = iota((16, CH), 0)
        t_core = t_acc[0:16] + t_acc[32:48]
        r_rows = jnp.concatenate(
            [r_acc[0:16] + r_acc[32:48], jnp.where(iota((8, 128), 0) == 0, r_acc[48:56], 0.0)], axis=0
        )
        r_rows = r_rows + pltpu.roll(r_rows, 96, 1)
        right = jnp.concatenate([centred, jnp.where(iota((8, CH), 0) == 0, 1.0, 0.0)], axis=0)
        corr = mm(r_rows, right, ((0,), (0,)), EXACT)[0:16] * (1.0 / CH)
        grad = (gain * t_core - corr) * HALF
        gain_grad = jnp.sum(centred * t_core, axis=0, keepdims=True) * HALF
        shift_grad = t_acc[48:49] * HALF
        sums = sums_ref[...]
        inv = 1.0 / small[14:15]
        grad = jnp.where(r16 == 11, gain_grad, grad)
        grad = jnp.where(r16 == 12, shift_grad, grad)
        grad = jnp.where(r16 == 13, jnp.sum(sums[0:8], axis=0, keepdims=True), grad)
        grad = jnp.where(r16 == 14, jnp.sum(sums[8:16], axis=0, keepdims=True) * inv, grad)
        grad = jnp.where(r16 == 15, jnp.sum(sums[16:24], axis=0, keepdims=True) * inv, grad)
        for q in range(4):
            small_own[q] = grad[:, q * 128 : (q + 1) * 128]
        for k in range(1, 4):
            sz_copy(k).start()

        rows16 = pl.ds(pl.multiple_of(core * 16, 16), 16)
        gathered[rows16, quarter] = f_sum[...]
        for k in range(1, DP):
            d_copy(k).wait_recv()
        second_grad[...] = gathered[...]
        value = small_own[zz]
        for k in range(1, 4):
            sz_copy(k).wait_recv()
            value = value + small_z[k]
        small_zsum[...] = value
        for k in range(1, 4):
            sx_copy(k).start()
        for m in range(4):
            pair_copy(m).wait_send()
        for k in range(1, 4):
            for copy in near_copies(k) + far_copies(k):
                copy.wait_send()
            y_copy(k).wait_send()
            sz_copy(k).wait_send()
        for k in range(1, 4):
            sx_copy(k).wait_recv()
            value = value + small_x[k]
        small_sum[...] = value
        for k in range(1, DP):
            e_copy(k).start()
        for k in range(1, DP):
            d_copy(k).wait_send()
        for k in range(1, 4):
            sx_copy(k).wait_send()
        for k in range(1, DP):
            e_copy(k).wait_recv()
            value = value + small_dp[k]
        for k in range(1, DP):
            e_copy(k).wait_send()
        vec_grad[...] = pltpu.roll(value, lax.rem(128 - lax.rem(fs, 4) * SHARD, 128), 1)


def last_kernel(feat_in, second_in, vec_in, feat_out, second_grad, first_grad, *rest):
    *vecs, stage, sems_in, sems_out = rest
    rows = [pl.ds(k * TILE, TILE) for k in range(STEPS)]
    loads = [pltpu.make_async_copy(feat_in.at[:, r], stage.at[:, r], sems_in.at[k]) for k, r in enumerate(rows)]
    stores = [pltpu.make_async_copy(stage.at[:, r], feat_out.at[:, r], sems_out.at[k]) for k, r in enumerate(rows)]
    for copy in loads:
        copy.start()
    for load, store in zip(loads, stores):
        load.wait()
        store.start()
    second_grad[...] = second_in[...]
    first_grad[...] = vec_in[0:TAPS, 0:SHARD]
    for at, ref in enumerate(vecs):
        ref[...] = vec_in[TAPS + at : TAPS + at + 1, 0:SHARD]
    for copy in stores:
        copy.wait()


def whole(shape):
    return pl.BlockSpec(shape, lambda i: (0,) * len(shape))


def local(
    waveforms, packing_list, segment_ids, first_weight, first_bias, first_gain, first_shift,
    second_weight, second_bias, second_gain, second_shift, cotangent,
):
    vecs = (first_bias, first_gain, first_shift, second_bias, second_gain, second_shift)
    vecs = [value.reshape(1, SHARD) for value in vecs]
    shape = jax.ShapeDtypeStruct
    dma = pltpu.SemaphoreType.DMA

    def block(i):
        return (0, jnp.clip(i - FIRST - 1, 0, STEPS - 1), 0)

    def vmem(kind, *dims):
        return pltpu.VMEM(dims, kind)

    features, second_grad, vec_grad = pl.pallas_call(
        main_kernel,
        grid=(SECOND + STEPS + 1,),
        out_shape=[shape((1, ROWS, CH), BF16), shape((SHARD, 3 * CH), F32), shape((16, 128), F32)],
        in_specs=[
            whole((4, 128)), whole((1, 128)), whole((320, FRAMES)), whole((TAPS, SHARD)),
            *([whole((1, SHARD))] * 6), whole((SHARD, 3 * CH)), pl.BlockSpec((1, TILE, CH), block),
        ],
        out_specs=[pl.BlockSpec((1, TILE, CH), block), whole((SHARD, 3 * CH)), whole((16, 128))],
        scratch_shapes=[
            vmem(BF16, 128, 320), vmem(BF16, 128, 320), vmem(BF16, 16, 128), vmem(BF16, 4, 16, 128),
            vmem(BF16, 16, 128), vmem(BF16, 4, 16, 128), vmem(BF16, 4, 4, SHARD, 3 * CH), vmem(F32, 144, 384),
            vmem(BF16, 128, CH), vmem(F32, 128, 256), vmem(BF16, TILE + 16, 384), vmem(BF16, 384, 384),
            vmem(BF16, STEPS, 2 * TILE, 128),
            vmem(F32, 16, CH), vmem(BF16, ROWS + 16, CH), vmem(BF16, ROWS, CH), vmem(BF16, ROWS, CH),
            vmem(BF16, ROWS, CH), vmem(BF16, ROWS, 128), vmem(BF16, ROWS, 128), vmem(BF16, ROWS, CH),
            vmem(BF16, ROWS, CH),
            vmem(F32, 8, CH), vmem(F32, CH, 3 * CH), vmem(F32, 24, CH), vmem(F32, TILE, CH), vmem(F32, TILE, CH),
            vmem(BF16, TILE, CH), vmem(BF16, TILE, CH), vmem(BF16, TILE, CH), vmem(BF16, TILE, CH),
            vmem(BF16, 4, 4, 2, 16, 3 * CH),
            vmem(F32, TILE, CH), vmem(F32, TILE, CH), vmem(F32, TILE, CH), vmem(F32, TILE, CH),
            vmem(BF16, 4, 4, 16, 3 * CH), vmem(BF16, 4, 4, 16, 3 * CH),
            vmem(BF16, 4, 4, 16, 768), vmem(BF16, 4, 4, 16, 768),
            vmem(BF16, 4, 16, 768), vmem(BF16, 4, 16, 768), vmem(BF16, 4, 16, 768), vmem(BF16, 4, 16, 768),
            vmem(F32, 16, 3 * CH), vmem(F32, 4, 16, 384), vmem(F32, 16, 384),
            vmem(F32, SHARD, 3 * CH), vmem(BF16, 128, CH), vmem(F32, 128, CH), vmem(F32, 128, 128),
            vmem(F32, 4, 16, 128), vmem(F32, 4, 16, 128), vmem(F32, 16, 128),
            vmem(F32, 4, 16, 128), vmem(F32, 16, 128), vmem(F32, DP, 16, 128),
            dma((DP,)), dma((DP,)), dma((4,)), dma((4,)), dma((4,)), dma((4,)),
            dma((2, 4)), dma((2, 4)), dma((2, 4)), dma((2, 4)), dma, dma,
            dma((4,)), dma((4,)), dma((2, 4)), dma((2, 4)), dma((2, 4)), dma((2, 4)),
            dma((4,)), dma((4,)), dma((DP,)), dma((DP,)),
            dma((4,)), dma((4,)), dma((4,)), dma((4,)), dma((DP,)), dma((DP,)),
        ],
        compiler_params=pltpu.CompilerParams(
            collective_id=0, has_side_effects=True, vmem_limit_bytes=VMEM_LIMIT
        ),
    )(packing_list, segment_ids, waveforms[0].T, first_weight.T, *vecs, second_weight, cotangent)

    one = shape((1, SHARD), F32)
    anywhere = pl.BlockSpec(memory_space=pl.ANY)
    local_vmem = pl.BlockSpec(memory_space=pltpu.VMEM)
    outs = pl.pallas_call(
        last_kernel,
        out_shape=[shape((1, ROWS, CH), BF16), shape((SHARD, 3 * CH), F32), shape((TAPS, SHARD), F32)] + [one] * 6,
        in_specs=[anywhere, local_vmem, local_vmem],
        out_specs=[anywhere] + [local_vmem] * 8,
        scratch_shapes=[pltpu.VMEM((1, ROWS, CH), BF16), dma((STEPS,)), dma((STEPS,))],
        compiler_params=pltpu.CompilerParams(vmem_limit_bytes=VMEM_LIMIT),
    )(features, second_grad, vec_grad)
    b1, n1, s1, b2, n2, s2 = [value.reshape(SHARD) for value in outs[3:]]
    return outs[0], outs[2].T, b1, n1, s1, outs[1], b2, n2, s2


def solution(mesh):
    placed = (
        P("dp", "fsdp", None), P(None, "fsdp"), P("dp", "fsdp"), P("fsdp", None), P("fsdp"), P("fsdp"),
        P("fsdp"), P("fsdp", None), P("fsdp"), P("fsdp"), P("fsdp"), P("dp", "fsdp", None),
    )
    out = (
        P("dp", "fsdp", None), P("fsdp", None), P("fsdp"), P("fsdp"), P("fsdp"), P("fsdp", None),
        P("fsdp"), P("fsdp"), P("fsdp"),
    )
    return jax.shard_map(local, mesh=mesh, in_specs=placed, out_specs=out, check_vma=False)
```

time: 539 us -> 99.4 us (0.18); the launches traced: 530 us -> 99.3 us
  other arithmetic: 166 us -> 0 us
  blocking collectives: 165 us -> 0 us
  local copies, waits for them, and re-layouts: 105 us -> 0 us
  Pallas kernels: 0 us -> 98.6 us
  matrix products: 52.8 us -> 0 us
  waiting for transfers between devices: 25.2 us -> 0 us
  between operations: 15.8 us -> 0.65 us
    reduce_sum x10 -> x0, other arithmetic: 102 us -> none  [the longest x2 57.2 us: norm_act(): scaled = centred * lax.rsqrt(spread + epsilon) * scale_by + shift_by]
    pallas_call x0 -> x2, Pallas kernels: none -> 98.6 us  [the longest x1 93.4 us: local(): pl.pallas_call(main_kernel, grid=(SECOND + STEPS + 1,), out_shape=[shape(...]
    unnamed x2 -> x0, blocking collectives: 93.4 us -> none
    reshape x3 -> x0, local copies, waits for them, and re-layouts: 49.1 us -> none  [the longest x2 35.8 us: local_pass(): grad_hidden = (grad_columns[:, :2 * channels] + jnp.concatenate([shifted,...]
    dot_general x4 -> x0, matrix products: 44.1 us -> none  [the longest x1 14.6 us: local_pass(): jnp.dot(grad_second, kernel_two, preferred_element_type=jnp.float32)]
    convert_element_type x9 -> x0, other arithmetic: 43.3 us -> none  [the longest x1 43.1 us: local_pass(): hidden = post_first.astype(jnp.bfloat16)]
    psum x1 -> x0, blocking collectives: 41 us -> none  [local(): lax.psum((second_part, summed[0], summed[1], summed[2], summed[3], summed...]
    all_gather x2 -> x0, blocking collectives: 30.7 us -> none  [the longest x1 15.4 us: local(): lax.all_gather(first_weight, 'fsdp', axis=0, tiled=True)]
  transfers between devices with their start and end apart: 4 -> 0, of which waited for: 2 -> 0; matrix products, arithmetic and copies ran while one was open for 49% -> 0% of each run, Pallas kernels for 0% -> 0%
where the time goes in v2:
time: 99.4 us; the launch traced here: 99.3 us
  Pallas kernels  98.6 us (99%)
    pallas_call x1, Pallas kernels, local(): pl.pallas_call(main_kernel, grid=(SECOND + STEPS + 1,), out_shape=[shape(...  93.4 us
    pallas_call x1, Pallas kernels, local(): pl.pallas_call(last_kernel, out_shape=[shape((1, ROWS, CH), BF16), shape(...  5.2 us

profile of v2, /device:TPU:1, one launch (start us, length us, event | category | flops | bytes accessed | tf_op | source)
XLA Modules:
  0.0 99.3 jit_solution(2774540640719025566)
XLA Ops:
  0.6 93.4 %shard_map.187 = (bf16[1,4096,512]{2,1,0:T(8,128)(2,1)}, f32[32,1536]{1,0:T(8,128)}, f32[16,128]{1,0:T(8,128)}) custom-call(s32[4,128]{1,0:T(4,128)} %list_ref.1, s32[1,128]{1,0:T(1,128)} %seg_ref.1, bf16[320,128]{1,0:T(8,128)(2,1)} %bitcast.17, bf16[10,32]{1,0:T(8,128)(2,1)} %bitcast.18, bf16[1,32]{1,0:T(2,128)(2,1)} %bitcast.19, bf16[1,32]{1,0:T(2,128)(2,1)} %bitcast.20, ...), custom_call_target="tpu_custom_call" | custom-call | tf_op jit(solution)/shard_map/pallas_call | solution.py:661
  94.1 5.2 %shard_map.188 = (bf16[1,4096,512]{2,1,0:T(8,128)(2,1)}, f32[32,1536]{1,0:T(8,128)}, f32[10,32]{1,0:T(8,128)}, f32[1,32]{1,0:T(1,128)}, f32[1,32]{1,0:T(1,128)},...) custom-call(bf16[1,4096,512]{2,1,0:T(8,128)(2,1)} %get-tuple-element.21.feat_in, ...), custom_call_target="tpu_custom_call" | custom-call | tf_op jit(solution)/shard_map/pallas_call | solution.py:703

commit v3 on v2

--- a/solution.py
+++ b/solution.py
@@ -10,9 +10,8 @@
 EXACT = lax.Precision.HIGHEST
 CH, FRAMES, ROWS, TILE, STEPS = 512, 128, 4096, 512, 8
 PER_STEP = TILE // 32
-PART = 256
+PART = 128
 VMEM_LIMIT = 60 << 20
-FIRST, SECOND = STEPS, 2 * STEPS + 2
 DP, FS = 8, 16
 SHARD, SLOT, TAPS = 32, 16, 10
 EPS = 1e-05
@@ -98,6 +97,14 @@
 def split(value):
     high = value.astype(BF16).astype(F32)
     return high, value - high
+
+
+def weave(*lists):
+    queue = []
+    for jobs in lists:
+        queue += [((at + 0.5) / len(jobs), job) for at, job in enumerate(jobs)]
+    for _, job in sorted(queue, key=lambda entry: entry[0]):
+        job()
 
 
 def tile_rows(index):
@@ -295,9 +302,8 @@
         )
         quad[:, 128:256] = jnp.where(row_at == 48, 1.0, 0.0)
 
-    @pl.when(step < STEPS)
-    def _():
-        patch_bf = patches[step]
+    def first_block(turn, _):
+        patch_bf = patches[turn]
         patch = patch_bf.astype(F32)
         form = mm(patch_bf, quad[...].astype(BF16), ((1,), (0,)))
         var = jnp.sum(form[:, 0:128] * patch, axis=1, keepdims=True)
@@ -306,7 +312,7 @@
         high, low = split(scaled)
         lane_t = iota((2 * TILE, 128), 1)
         left = jnp.where(lane_t < 32, high, jnp.where(lane_t < 48, low, patch)).astype(BF16)
-        rows = tile_rows(step)
+        rows = tile_rows(turn)
         for part, (h_ref, d_ref, l_ref) in enumerate(((he, de, le), (ho, do, lo))):
             piece = left[part * TILE : (part + 1) * TILE]
             l_ref[rows] = piece
@@ -315,26 +321,23 @@
             h_ref[rows] = (u * phi).astype(BF16)
             bell = jnp.exp2(u * u * EXP_BY + EXP_PLUS)
             d_ref[rows] = (phi + u * bell).astype(BF16)
-
-    @pl.when(step == 1)
+        return 0
+
+    @pl.when(step == 0)
     def _():
+        lax.fori_loop(0, 2, first_block, 0)
         for k in range(1, 4):
             for copy in near_weights(k):
                 copy.wait_recv()
         for k in range(1, 4):
             for copy in far_weights(k):
                 copy.start()
-
-    @pl.when(step == STEPS - 3)
-    def _():
+        lax.fori_loop(2, 6, first_block, 0)
         for k in range(1, 4):
             for copy in far_weights(k):
                 copy.wait_recv()
         forward_copy().start()
-
-    @pl.when(step == STEPS - 1)
-    def _():
-        forward_copy().wait_recv()
+        lax.fori_loop(6, STEPS, first_block, 0)
         for k in range(1, DP):
             a2a_copy(k).wait_send()
         for k in range(1, 4):
@@ -342,6 +345,7 @@
             part_z(k).wait_send()
             for copy in near_weights(k) + far_weights(k):
                 copy.wait_send()
+        forward_copy().wait_recv()
         forward_copy().wait_send()
 
     def pair_copy(m):
@@ -383,30 +387,46 @@
     def e_copy(k):
         return send(small_sum, small_dp.at[k], e_s.at[k], e_r.at[k], (lax.rem(dp + k, DP), fs))
 
-    def taps(c):
-        return second_all[:, :, :, c * CH : (c + 1) * CH].reshape(CH, CH)
+    def taps(c, n=None):
+        if n is None:
+            return second_all[:, :, :, c * CH : (c + 1) * CH].reshape(CH, CH)
+        return second_all[2 * n : 2 * n + 2, :, :, c * CH : (c + 1) * CH].reshape(CH // 2, CH)
 
     def convolve(slot):
-        rows = tile_rows(step - FIRST)
-        more = pl.ds(pl.multiple_of((step - FIRST) * TILE, TILE), TILE + 16)
-        pre = mm(he[rows], taps(0), ((1,), (1,))) + mm(ho[rows], taps(1), ((1,), (1,)))
-        third = mm(he[more], taps(2), ((1,), (1,)))
-        pres[slot][...] = pre + pltpu.roll(third, TILE + 15, 0)[:TILE]
+        rows = tile_rows(step)
+        more = pl.ds(pl.multiple_of((step) * TILE, TILE), TILE + 16)
+        kept = {}
+
+        def third():
+            kept[0] = pltpu.roll(mm(he[more], taps(2), ((1,), (1,))), TILE + 15, 0)[:TILE]
+
+        def first():
+            kept[1] = mm(he[rows], taps(0), ((1,), (1,)))
+
+        def rest():
+            pres[slot][...] = kept[1] + mm(ho[rows], taps(1), ((1,), (1,))) + kept[0]
+
+        return [third, first, rest]
 
     def activate(slot):
         bias, gain, shift = small_ref[13:14], small_ref[14:15], small_ref[15:16]
         gain_u, shift_u = gain * HALF, shift * HALF
-        last = carry[0:1]
-        totals = [jnp.zeros((8, CH), F32)] * 3
-        for part in range(TILE // PART):
+        state = {"last": carry[0:1]}
+
+        def norms(part):
             rows = pl.ds(part * PART, PART)
-            far = pl.ds(pl.multiple_of((step - FIRST - 1) * TILE + part * PART, PART), PART)
-            keep = lo[far].astype(F32)[:, 48:49]
             pre = pres[slot][rows] + bias
             centred = pre - jnp.mean(pre, axis=1, keepdims=True)
             var = jnp.mean(centred * centred, axis=1, keepdims=True)
             scale = lax.rsqrt(var + EPS)
             norm = centred * scale
+            state[part] = (norm, scale)
+
+        def slopes(part):
+            rows = pl.ds(part * PART, PART)
+            far = pl.ds(pl.multiple_of((step - 1) * TILE + part * PART, PART), PART)
+            keep = lo[far].astype(F32)[:, 48:49]
+            norm, scale = state[part]
             u = norm * gain_u + shift_u
             phi = HALF * lax.erf(u) + HALF
             feat_ref[0, rows] = (u * phi * keep).astype(BF16)
@@ -416,69 +436,99 @@
             prod = dnorm * norm
             mean_a = jnp.mean(dnorm, axis=1, keepdims=True)
             mean_b = jnp.mean(prod, axis=1, keepdims=True)
+            state[part, 1] = (norm, scale, dnorm, prod, mean_a, mean_b)
+
+        def finish(part):
+            rows = pl.ds(part * PART, PART)
+            far = pl.ds(pl.multiple_of((step - 1) * TILE + part * PART, PART), PART)
+            norm, scale, dnorm, prod, mean_a, mean_b = state[part, 1]
             dpre = (dnorm - mean_a - norm * mean_b) * scale
             for at, value in enumerate((dpre, prod, dnorm)):
-                totals[at] = totals[at] + jnp.sum(value.reshape(PART // 8, 8, CH), axis=0)
-            g1[far] = dpre.astype(BF16)
-            gs_pair[slot][0][rows] = dpre.astype(BF16)
+                sums_ref[at * 8 : at * 8 + 8] += jnp.sum(value.reshape(PART // 8, 8, CH), axis=0)
+            here = dpre.astype(BF16)
+            g1[far] = here
+            gs_pair[slot][0][rows] = here
             rolled = pltpu.roll(dpre, 1, 0)
-            rolled = jnp.where(iota((PART, CH), 0) == 0, last, rolled).astype(BF16)
+            rolled = jnp.where(iota((PART, CH), 0) == 0, state["last"], rolled).astype(BF16)
             gs[far] = rolled
             gs_pair[slot][1][rows] = rolled
-            last = dpre[PART - 1 : PART]
-        carry[0:1] = last
-        for at in range(3):
-            sums_ref[at * 8 : at * 8 + 8] += totals[at]
+            state["last"] = dpre[PART - 1 : PART]
+            if part == TILE // PART - 1:
+                carry[0:1] = state["last"]
+
+        jobs = []
+        count = TILE // PART
+        for turn in range(count + 2):
+            for lag, job in ((0, norms), (1, slopes), (2, finish)):
+                if 0 <= turn - lag < count:
+                    jobs.append(lambda job=job, part=turn - lag: job(part))
+        return jobs
 
     def weigh(slot):
         g_part, gs_part = gs_pair[slot]
-        rows = tile_rows(step - FIRST - 2)
-        for c, (left, right) in enumerate(((g_part, he), (g_part, ho), (gs_part, he))):
-            total[:, c * CH : (c + 1) * CH] += mm(left[...], right[rows], ((0,), (0,)))
-
-    at = step - FIRST
-
-    @pl.when(at == 0)
+        rows = tile_rows(step - 2)
+
+        def run(c, n):
+            left, right = ((g_part, he), (g_part, ho), (gs_part, he))[c]
+            cols = slice(n * 256, n * 256 + 256)
+            total[:, c * CH + n * 256 : c * CH + n * 256 + 256] += mm(left[...], right[rows, cols], ((0,), (0,)))
+
+        return [lambda c=c, n=n: run(c, n) for c in range(3) for n in range(2)]
+
+    @pl.when(step == 0)
     def _():
-        convolve(0)
-
-    @pl.when(at == 1)
+        weave(convolve(0))
+
+    @pl.when(step == 1)
     def _():
-        convolve(1)
-        activate(0)
+        weave(convolve(1), activate(0))
 
     for slot in range(2):
 
-        @pl.when((at >= 2) & (at < STEPS) & (at % 2 == slot))
+        @pl.when((step >= 2) & (step < STEPS) & (step % 2 == slot))
         def _(slot=slot):
-            convolve(slot)
-            weigh(slot)
-            activate(1 - slot)
-
-    @pl.when(at == STEPS)
+            weave(convolve(slot) + weigh(slot), activate(1 - slot))
+
+    @pl.when(step == STEPS)
     def _():
-        weigh(0)
-        activate(1)
-
-    @pl.when(at == STEPS + 1)
+        weave(weigh(0), activate(1))
+
+    @pl.when(step == STEPS + 1)
     def _():
-        weigh(1)
+        weave(weigh(1))
         grad_ref[...] = total[...].astype(BF16).reshape(4, 4, 2, 16, 3 * CH)
         for m in range(4):
             pair_copy(m).start()
 
-    def spread(slot):
-        rows = tile_rows(step - SECOND)
-        g_tile = g1[rows]
-        even = mm(g_tile, taps(0), ((1,), (0,)))
-        spreads[slot][0][...] = even + mm(gs[rows], taps(2), ((1,), (0,)))
-        spreads[slot][1][...] = mm(g_tile, taps(1), ((1,), (0,)))
-
-    def gather_terms(slot):
-        lane = iota((TILE, 128), 1)
-        rows = tile_rows(step - SECOND - 1)
-        for d_hidden, slope, lhs in zip(spreads[slot], (de, do), (le, lo)):
-            ds = (d_hidden[...] * slope[rows].astype(F32)).astype(BF16)
+    def spread(slot, turn):
+        rows = tile_rows(turn)
+
+        kept = {}
+
+        def even(n):
+            cols = slice(n * 256, n * 256 + 256)
+            kept[n] = mm(g1[rows], taps(0)[:, cols], ((1,), (0,)))
+
+        def more(n):
+            cols = slice(n * 256, n * 256 + 256)
+            spreads[slot][0][:, cols] = kept[n] + mm(gs[rows], taps(2)[:, cols], ((1,), (0,)))
+
+        def odd(n):
+            cols = slice(n * 256, n * 256 + 256)
+            spreads[slot][1][:, cols] = mm(g1[rows], taps(1)[:, cols], ((1,), (0,)))
+
+        order = ((even, 0), (more, 0), (even, 1), (more, 1), (odd, 0), (odd, 1))
+        return [lambda job=job, n=n: job(n) for job, n in order]
+
+    def gather_terms(slot, turn):
+        size = TILE
+        lane = iota((size, 128), 1)
+
+        def run(parity, part):
+            near = pl.ds(part * size, size)
+            rows = pl.ds(pl.multiple_of(turn * TILE + part * size, size), size)
+            slope, lhs = ((de, le), (do, lo))[parity]
+            ds = (spreads[slot][parity][near] * slope[rows].astype(F32)).astype(BF16)
             left = lhs[rows]
             left_f = left.astype(F32)
             z = mm(ds, wz[...], ((1,), (1,)))
@@ -488,36 +538,33 @@
             t_acc[...] += mm(left, ds, ((0,), (0,)))
             r_acc[...] += mm(y, left, ((0,), (0,)))
 
-    then = step - SECOND
-
-    @pl.when(then == 0)
+        return [lambda a=a, b=b: run(a, b) for a in range(2) for b in range(1)]
+
+    @pl.when(step == STEPS + 1)
     def _():
+        def both(slot, turn):
+            weave(spread(slot, turn), gather_terms(1 - slot, turn - 1))
+
+        def pair(turn, _):
+            both(0, 2 * turn)
+            both(1, 2 * turn + 1)
+            return 0
+
         small = small_ref[...]
         gain = small[11:12]
         high, low = split(centred_weights(small) * gain)
         wz[...] = jnp.concatenate(
             [high, low, high, jnp.where(iota((16, CH), 0) == 0, gain, 0.0), jnp.zeros((64, CH), F32)], axis=0
         ).astype(BF16)
-        spread(0)
-
-    for slot in range(2):
-
-        @pl.when((then >= 1) & (then < STEPS) & (then % 2 == slot))
-        def _(slot=slot):
-            spread(slot)
-            gather_terms(1 - slot)
-
-    @pl.when(then == 1)
-    def _():
+        weave(spread(0, 0))
+        both(1, 1)
         for m in range(4):
             pair_copy(m).wait_recv()
             pair_sum[m] = (grad_ref[m, :, core].astype(F32) + pair_in[m].astype(F32)).astype(BF16)
         for k in range(1, 4):
             for copy in near_copies(k):
                 copy.start()
-
-    @pl.when(then == 5)
-    def _():
+        lax.fori_loop(1, 3, pair, 0)
         value_a = pair_sum[zz, :, :, cols_a].astype(F32)
         value_b = pair_sum[:, xx, :, cols_b].astype(F32)
         for k in range(1, 4):
@@ -530,9 +577,7 @@
         for k in range(1, 4):
             for copy in far_copies(k):
                 copy.start()
-
-    @pl.when(then == 6)
-    def _():
+        both(0, 6)
         value_a = sum_a[xx].astype(F32)
         value_b = sum_b[zz].astype(F32)
         for k in range(1, 4):
@@ -544,9 +589,7 @@
         f_all[:, cols_b] = value_b
         for k in range(1, 4):
             y_copy(k).start()
-
-    @pl.when(then == 7)
-    def _():
+        both(1, 7)
         value = f_all[:, quarter]
         for k in range(1, 4):
             y_copy(k).wait_recv()
@@ -554,10 +597,7 @@
         f_sum[...] = value
         for k in range(1, DP):
             d_copy(k).start()
-
-    @pl.when(then == STEPS)
-    def _():
-        gather_terms(1)
+        weave(gather_terms(1, STEPS - 1))
         small = small_ref[...]
         centred = centred_weights(small)
         gain = small[11:12]
@@ -653,14 +693,14 @@
     dma = pltpu.SemaphoreType.DMA
 
     def block(i):
-        return (0, jnp.clip(i - FIRST - 1, 0, STEPS - 1), 0)
+        return (0, jnp.clip(i - 1, 0, STEPS - 1), 0)
 
     def vmem(kind, *dims):
         return pltpu.VMEM(dims, kind)
 
     features, second_grad, vec_grad = pl.pallas_call(
         main_kernel,
-        grid=(SECOND + STEPS + 1,),
+        grid=(STEPS + 2,),
         out_shape=[shape((1, ROWS, CH), BF16), shape((SHARD, 3 * CH), F32), shape((16, 128), F32)],
         in_specs=[
             whole((4, 128)), whole((1, 128)), whole((320, FRAMES)), whole((TAPS, SHARD)),

time: 99.4 us -> 91.7 us (0.923)
  Pallas kernels: 98.6 us -> 90.9 us
    pallas_call x1, Pallas kernels: 93.4 us -> 85.7 us  [local(): pl.pallas_call(main_kernel, grid=(STEPS + 2,), out_shape=[shape((1, ROWS,...]
where the time goes in v3:
time: 91.7 us; the launch traced here: 91.5 us
  Pallas kernels  90.9 us (99%)
    pallas_call x1, Pallas kernels, local(): pl.pallas_call(main_kernel, grid=(STEPS + 2,), out_shape=[shape((1, ROWS,...  85.7 us
    pallas_call x1, Pallas kernels, local(): pl.pallas_call(last_kernel, out_shape=[shape((1, ROWS, CH), BF16), shape(...  5.2 us

profile of v3, /device:TPU:1, one launch (start us, length us, event | category | flops | bytes accessed | tf_op | source)
XLA Modules:
  0.0 91.5 jit_solution(11012952823561245953)
XLA Ops:
  0.6 85.7 %shard_map.187 = (bf16[1,4096,512]{2,1,0:T(8,128)(2,1)}, f32[32,1536]{1,0:T(8,128)}, f32[16,128]{1,0:T(8,128)}) custom-call(s32[4,128]{1,0:T(4,128)} %list_ref.1, s32[1,128]{1,0:T(1,128)} %seg_ref.1, bf16[320,128]{1,0:T(8,128)(2,1)} %bitcast.17, bf16[10,32]{1,0:T(8,128)(2,1)} %bitcast.18, bf16[1,32]{1,0:T(2,128)(2,1)} %bitcast.19, bf16[1,32]{1,0:T(2,128)(2,1)} %bitcast.20, ...), custom_call_target="tpu_custom_call" | custom-call | tf_op jit(solution)/shard_map/pallas_call | solution.py:701
  86.3 5.2 %shard_map.188 = (bf16[1,4096,512]{2,1,0:T(8,128)(2,1)}, f32[32,1536]{1,0:T(8,128)}, f32[10,32]{1,0:T(8,128)}, f32[1,32]{1,0:T(1,128)}, f32[1,32]{1,0:T(1,128)},...) custom-call(bf16[1,4096,512]{2,1,0:T(8,128)(2,1)} %get-tuple-element.21.feat_in, ...), custom_call_target="tpu_custom_call" | custom-call | tf_op jit(solution)/shard_map/pallas_call | solution.py:743

commit v4 on v3

--- a/solution.py
+++ b/solution.py
@@ -265,11 +265,9 @@
         frames[0:128, 0:320] = packed
         frames[128:144, :] = jnp.zeros((16, 384), F32)
         def cut(turn, _):
-            few = frames[pl.ds(pl.multiple_of(turn * PER_STEP, PER_STEP), 32)].astype(BF16)
-            spread = iota((TILE + 16, 32), 0)
-            start = iota((TILE + 16, 32), 1) * 32
-            repeat = jnp.where((spread >= start) & (spread < start + 32), 1.0, 0.0).astype(BF16)
-            wide = mm(repeat, few, ((1,), (0,))).astype(BF16) * mask_ref[...]
+            few = frames[pl.ds(pl.multiple_of(turn * PER_STEP, PER_STEP), PER_STEP + 8)]
+            spread = jnp.broadcast_to(few[:, None], (PER_STEP + 8, 32, 384)).reshape(TILE + 256, 384)
+            wide = spread[: TILE + 16].astype(BF16) * mask_ref[...]
             taken = mm(wide, pick_ref[...], ((1,), (0,)))
             even = taken[:TILE, 0:128]
             odd = taken[:TILE, 128:256] + pltpu.roll(taken[:, 256:384], TILE + 15, 0)[:TILE]
@@ -279,6 +277,12 @@
             return 0
 
         lax.fori_loop(0, STEPS, cut, 0)
+        for k in range(1, 4):
+            for copy in near_weights(k):
+                copy.wait_recv()
+        for k in range(1, 4):
+            for copy in far_weights(k):
+                copy.start()
 
         part_rows[pl.ds(zz, 1)] = part_row[...][None]
         for k in range(1, 4):
@@ -325,14 +329,7 @@
 
     @pl.when(step == 0)
     def _():
-        lax.fori_loop(0, 2, first_block, 0)
-        for k in range(1, 4):
-            for copy in near_weights(k):
-                copy.wait_recv()
-        for k in range(1, 4):
-            for copy in far_weights(k):
-                copy.start()
-        lax.fori_loop(2, 6, first_block, 0)
+        lax.fori_loop(0, 6, first_block, 0)
         for k in range(1, 4):
             for copy in far_weights(k):
                 copy.wait_recv()
@@ -578,6 +575,7 @@
             for copy in far_copies(k):
                 copy.start()
         both(0, 6)
+        both(1, 7)
         value_a = sum_a[xx].astype(F32)
         value_b = sum_b[zz].astype(F32)
         for k in range(1, 4):
@@ -589,14 +587,6 @@
         f_all[:, cols_b] = value_b
         for k in range(1, 4):
             y_copy(k).start()
-        both(1, 7)
-        value = f_all[:, quarter]
-        for k in range(1, 4):
-            y_copy(k).wait_recv()
-            value = value + y_in[k]
-        f_sum[...] = value
-        for k in range(1, DP):
-            d_copy(k).start()
         weave(gather_terms(1, STEPS - 1))
         small = small_ref[...]
         centred = centred_weights(small)
@@ -623,12 +613,16 @@
             small_own[q] = grad[:, q * 128 : (q + 1) * 128]
         for k in range(1, 4):
             sz_copy(k).start()
+        value = f_all[:, quarter]
+        for k in range(1, 4):
+            y_copy(k).wait_recv()
+            value = value + y_in[k]
+        f_sum[...] = value
+        for k in range(1, DP):
+            d_copy(k).start()
 
         rows16 = pl.ds(pl.multiple_of(core * 16, 16), 16)
         gathered[rows16, quarter] = f_sum[...]
-        for k in range(1, DP):
-            d_copy(k).wait_recv()
-        second_grad[...] = gathered[...]
         value = small_own[zz]
         for k in range(1, 4):
             sz_copy(k).wait_recv()
@@ -649,6 +643,9 @@
         small_sum[...] = value
         for k in range(1, DP):
             e_copy(k).start()
+        for k in range(1, DP):
+            d_copy(k).wait_recv()
+        second_grad[...] = gathered[...]
         for k in range(1, DP):
             d_copy(k).wait_send()
         for k in range(1, 4):

time: 91.7 us -> 85 us (0.927)
  Pallas kernels: 90.9 us -> 84.1 us
    pallas_call x1, Pallas kernels: 85.7 us -> 78.9 us  [local(): pl.pallas_call(main_kernel, grid=(STEPS + 2,), out_shape=[shape((1, ROWS,...]
where the time goes in v4:
time: 85 us; the launch traced here: 84.8 us
  Pallas kernels  84.1 us (99%)
    pallas_call x1, Pallas kernels, local(): pl.pallas_call(main_kernel, grid=(STEPS + 2,), out_shape=[shape((1, ROWS,...  78.9 us
    pallas_call x1, Pallas kernels, local(): pl.pallas_call(last_kernel, out_shape=[shape((1, ROWS, CH), BF16), shape(...  5.2 us

profile of v4, /device:TPU:1, one launch (start us, length us, event | category | flops | bytes accessed | tf_op | source)
XLA Modules:
  0.0 84.8 jit_solution(13391316036093739835)
XLA Ops:
  0.6 78.9 %shard_map.187 = (bf16[1,4096,512]{2,1,0:T(8,128)(2,1)}, f32[32,1536]{1,0:T(8,128)}, f32[16,128]{1,0:T(8,128)}) custom-call(s32[4,128]{1,0:T(4,128)} %list_ref.1, s32[1,128]{1,0:T(1,128)} %seg_ref.1, bf16[320,128]{1,0:T(8,128)(2,1)} %bitcast.17, bf16[10,32]{1,0:T(8,128)(2,1)} %bitcast.18, bf16[1,32]{1,0:T(2,128)(2,1)} %bitcast.19, bf16[1,32]{1,0:T(2,128)(2,1)} %bitcast.20, ...), custom_call_target="tpu_custom_call" | custom-call | tf_op jit(solution)/shard_map/pallas_call | solution.py:698
  79.6 5.2 %shard_map.188 = (bf16[1,4096,512]{2,1,0:T(8,128)(2,1)}, f32[32,1536]{1,0:T(8,128)}, f32[10,32]{1,0:T(8,128)}, f32[1,32]{1,0:T(1,128)}, f32[1,32]{1,0:T(1,128)},...) custom-call(bf16[1,4096,512]{2,1,0:T(8,128)(2,1)} %get-tuple-element.21.feat_in, ...), custom_call_target="tpu_custom_call" | custom-call | tf_op jit(solution)/shard_map/pallas_call | solution.py:740

commit v5 on v4

--- a/solution.py
+++ b/solution.py
@@ -117,7 +117,7 @@
     slots, heard, part_own, smalls, part_row, part_rows, second_all, frames, rhs, quad, mask_ref, pick_ref, patches,
     small_ref, he, ho, de, do, le, lo, g1, gs,
     carry, total, sums_ref, pre_0, pre_1, g_0, g_1, gs_0, gs_1, grad_ref,
-    even_0, even_1, odd_0, odd_1, pair_in, pair_sum, near_a, near_b, sum_a, sum_b,
+    even_1, odd_1, pair_in, pair_sum, near_a, near_b, sum_a, sum_b,
     far_a, far_b, f_all, y_in, f_sum, gathered, wz, t_acc, r_acc,
     small_own, small_z, small_zsum, small_x, small_sum, small_dp,
     a2a_s, a2a_r, sm_s, sm_r, sz_0, sz_1, w_s, w_r, v_s, v_r, fw_s, fw_r,
@@ -132,7 +132,7 @@
     half = pl.ds(pl.multiple_of(core * 768, 128), 768)
     quarter = pl.ds(pl.multiple_of(yy * 384, 128), 384)
     pres, gs_pair = (pre_0, pre_1), ((g_0, gs_0), (g_1, gs_1))
-    spreads = ((even_0, odd_0), (even_1, odd_1))
+    spreads = ((pre_0, pre_1), (even_1, odd_1))
 
     def a2a_copy(k):
         target = lax.rem(dp + k, DP)
@@ -276,7 +276,7 @@
             patches[turn] = (jnp.concatenate([even, odd], axis=0) + bias_lane).astype(BF16)
             return 0
 
-        lax.fori_loop(0, STEPS, cut, 0)
+        lax.fori_loop(0, STEPS, cut, 0, unroll=2)
         for k in range(1, 4):
             for copy in near_weights(k):
                 copy.wait_recv()
@@ -329,12 +329,12 @@
 
     @pl.when(step == 0)
     def _():
-        lax.fori_loop(0, 6, first_block, 0)
+        lax.fori_loop(0, 6, first_block, 0, unroll=2)
         for k in range(1, 4):
             for copy in far_weights(k):
                 copy.wait_recv()
         forward_copy().start()
-        lax.fori_loop(6, STEPS, first_block, 0)
+        lax.fori_loop(6, STEPS, first_block, 0, unroll=2)
         for k in range(1, DP):
             a2a_copy(k).wait_send()
         for k in range(1, 4):
@@ -715,7 +715,7 @@
             vmem(F32, 8, CH), vmem(F32, CH, 3 * CH), vmem(F32, 24, CH), vmem(F32, TILE, CH), vmem(F32, TILE, CH),
             vmem(BF16, TILE, CH), vmem(BF16, TILE, CH), vmem(BF16, TILE, CH), vmem(BF16, TILE, CH),
             vmem(BF16, 4, 4, 2, 16, 3 * CH),
-            vmem(F32, TILE, CH), vmem(F32, TILE, CH), vmem(F32, TILE, CH), vmem(F32, TILE, CH),
+            vmem(F32, TILE, CH), vmem(F32, TILE, CH),
             vmem(BF16, 4, 4, 16, 3 * CH), vmem(BF16, 4, 4, 16, 3 * CH),
             vmem(BF16, 4, 4, 16, 768), vmem(BF16, 4, 4, 16, 768),
             vmem(BF16, 4, 16, 768), vmem(BF16, 4, 16, 768), vmem(BF16, 4, 16, 768), vmem(BF16, 4, 16, 768),

time: 85 us -> 83.4 us (0.981)
  Pallas kernels: 84.1 us -> 82.6 us
    pallas_call x1, Pallas kernels: 78.9 us -> 77.4 us  [local(): pl.pallas_call(main_kernel, grid=(STEPS + 2,), out_shape=[shape((1, ROWS,...]
where the time goes in v5:
time: 83.4 us; the launch traced here: 83.3 us
  Pallas kernels  82.6 us (99%)
    pallas_call x1, Pallas kernels, local(): pl.pallas_call(main_kernel, grid=(STEPS + 2,), out_shape=[shape((1, ROWS,...  77.4 us
    pallas_call x1, Pallas kernels, local(): pl.pallas_call(last_kernel, out_shape=[shape((1, ROWS, CH), BF16), shape(...  5.2 us

profile of v5, /device:TPU:1, one launch (start us, length us, event | category | flops | bytes accessed | tf_op | source)
XLA Modules:
  0.0 83.3 jit_solution(15960351614724577506)
XLA Ops:
  0.6 77.4 %shard_map.187 = (bf16[1,4096,512]{2,1,0:T(8,128)(2,1)}, f32[32,1536]{1,0:T(8,128)}, f32[16,128]{1,0:T(8,128)}) custom-call(s32[4,128]{1,0:T(4,128)} %list_ref.1, s32[1,128]{1,0:T(1,128)} %seg_ref.1, bf16[320,128]{1,0:T(8,128)(2,1)} %bitcast.17, bf16[10,32]{1,0:T(8,128)(2,1)} %bitcast.18, bf16[1,32]{1,0:T(2,128)(2,1)} %bitcast.19, bf16[1,32]{1,0:T(2,128)(2,1)} %bitcast.20, ...), custom_call_target="tpu_custom_call" | custom-call | tf_op jit(solution)/shard_map/pallas_call | solution.py:698
  78.1 5.2 %shard_map.188 = (bf16[1,4096,512]{2,1,0:T(8,128)(2,1)}, f32[32,1536]{1,0:T(8,128)}, f32[10,32]{1,0:T(8,128)}, f32[1,32]{1,0:T(1,128)}, f32[1,32]{1,0:T(1,128)},...) custom-call(bf16[1,4096,512]{2,1,0:T(8,128)(2,1)} %get-tuple-element.21.feat_in, ...), custom_call_target="tpu_custom_call" | custom-call | tf_op jit(solution)/shard_map/pallas_call | solution.py:740
